TPU v7x, 256 devices: a whole 4x4x8 slice. The times are simulated.
256 devices in a mesh: seq: 64 (over x, z, core), head: 4 (over y).
Axes of the slice: x: 4, y: 4, z: 8, core: 2. Of those that a mesh axis runs over, the one named last changes fastest.
Arguments:
- queries: bfloat16 [49152, 4096], P('seq', 'head')
- keys: bfloat16 [49152, 4096], P('seq', 'head'), may hold values from -4 to 4
- values: bfloat16 [49152, 4096], P('seq', 'head')
- cotangent: bfloat16 [49152, 4096], P('seq', 'head'), may hold values from -6 to 6
- norm_gain: float32 [4096], P('head'), may hold values from 0.1 to 1.9
- doc_start: int32 [49152], P('seq'), may hold values from 0 to 48896, as said below
Outputs:
- normed: bfloat16 [49152, 4096], P('seq', 'head')
- grad_queries: bfloat16 [49152, 4096], P('seq', 'head')
- grad_keys: bfloat16 [49152, 4096], P('seq', 'head')
- grad_values: bfloat16 [49152, 4096], P('seq', 'head')
Inputs may be any that keep to these rules, and one draw needn't show every extreme that they name: doc_start[t] is the start of t's document: a multiple of 256, at most t, equal for all tokens of a document, and equal to t at each document's first token. Every document touches at most 16 consecutive blocks of 768 tokens, and in every draw some document touches exactly 16 blocks. The last 256 tokens form a document of their own.
All inputs are finite; a program needn't handle non-finite values.
Results may differ from a plain program's by a relative error of at most 0.0058.
Values sent between devices are 32-bit elements; how exact they have to be, the bound alone decides.
No kernel may reach another device: no remote copies, remote signals or barrier semaphores. Data moves between devices by JAX's collectives and lax.ppermute only.
A program may use at most 192 MiB of HBM per device.

v0:
```python
import jax
import jax.numpy as jnp
from jax import lax
from jax.sharding import PartitionSpec as P

HEAD_DIM = 128


epsilon = 1e-06


def prefix(part, axis, combine, identity, reverse):
    count = lax.axis_size(axis)
    place = lax.axis_index(axis)
    ahead = count - 1 - place if reverse else place
    gathered = jax.tree.map(lambda a: lax.all_gather(a, axis), part)
    state = jax.tree.map(lambda a, e: jnp.zeros_like(a) + jnp.asarray(e, a.dtype), part, identity)

    def one(step, state):
        source = count - 1 - step if reverse else step
        return combine(
            state, jax.tree.map(lambda a: lax.dynamic_index_in_dim(a, source, 0, False), gathered)
        )

    return lax.fori_loop(0, ahead, one, state)


def combine(earlier, later):
    early_flag, early_state = earlier
    late_flag, late_state = later
    return (jnp.maximum(early_flag, late_flag), late_state + (1.0 - late_flag) * early_state)


def on_device(queries, keys, values, cotangent, norm_gain, doc_start):
    tokens = queries.shape[0]
    local_width = queries.shape[1]
    heads_here = local_width // HEAD_DIM

    def shaped(data):
        return data.reshape(tokens, heads_here, HEAD_DIM)

    query_h = shaped(queries)
    key_h = shaped(keys)
    value_h = shaped(values)
    offset = lax.axis_index("seq") * tokens
    position = jnp.arange(tokens, dtype=jnp.int32)
    same_doc = (doc_start[:, None] == doc_start[None, :]) & (position[:, None] >= position[None, :])
    begins = jnp.any(doc_start == offset + position).astype(jnp.float32)
    carried = doc_start < offset
    closing = doc_start == doc_start[-1]
    scores = jnp.einsum("thd,shd->hts", query_h, key_h, preferred_element_type=jnp.float32)
    attend = jnp.where(same_doc[None], scores, 0.0).astype(jnp.bfloat16)
    tail_state = jnp.einsum(
        "thd,the->hde",
        jnp.where(closing[:, None, None], key_h, 0),
        value_h,
        preferred_element_type=jnp.float32,
    )
    zero_state = jnp.zeros_like(tail_state)
    zero_flag = jnp.zeros((), jnp.float32)
    enter_flag, enter_state = prefix(
        (begins, tail_state), "seq", combine, (zero_flag, zero_state), False
    )
    prefix_bf = enter_state.astype(jnp.bfloat16)
    attended = jnp.einsum("hts,she->the", attend, value_h, preferred_element_type=jnp.float32)
    attended = attended + jnp.where(
        carried[:, None, None],
        jnp.einsum("thd,hde->the", query_h, prefix_bf, preferred_element_type=jnp.float32),
        0.0,
    )
    flat_out = attended.reshape(tokens, local_width)
    scaled = norm_gain[None, :] * cotangent.astype(jnp.float32)
    square_sum, cross_sum = lax.psum(
        (jnp.sum(flat_out * flat_out, axis=1), jnp.sum(scaled * flat_out, axis=1)), "head"
    )
    features = local_width * lax.axis_size("head")
    inverse = lax.rsqrt(square_sum / features + epsilon)
    normed = (flat_out * inverse[:, None] * norm_gain[None, :]).astype(jnp.bfloat16)
    grad_flat = inverse[:, None] * (
        scaled - flat_out * (inverse * inverse * cross_sum / features)[:, None]
    )
    grad_out = grad_flat.astype(jnp.bfloat16).reshape(tokens, heads_here, HEAD_DIM)
    head_state = jnp.einsum(
        "thd,the->hde",
        jnp.where(carried[:, None, None], query_h, 0),
        grad_out,
        preferred_element_type=jnp.float32,
    )
    after_flag, after_state = prefix(
        (begins, head_state), "seq", combine, (zero_flag, zero_state), True
    )
    after_bf = after_state.astype(jnp.bfloat16)
    back_scores = jnp.einsum("the,she->hts", grad_out, value_h, preferred_element_type=jnp.float32)
    backs = jnp.where(same_doc[None], back_scores, 0.0).astype(jnp.bfloat16)
    grad_q = jnp.einsum("hts,shd->thd", backs, key_h, preferred_element_type=jnp.float32)
    grad_q = grad_q + jnp.where(
        carried[:, None, None],
        jnp.einsum("the,hde->thd", grad_out, prefix_bf, preferred_element_type=jnp.float32),
        0.0,
    )
    grad_k = jnp.einsum("hts,thd->shd", backs, query_h, preferred_element_type=jnp.float32)
    grad_k = grad_k + jnp.where(
        closing[:, None, None],
        jnp.einsum("she,hde->shd", value_h, after_bf, preferred_element_type=jnp.float32),
        0.0,
    )
    grad_v = jnp.einsum("hts,the->she", attend, grad_out, preferred_element_type=jnp.float32)
    grad_v = grad_v + jnp.where(
        closing[:, None, None],
        jnp.einsum("shd,hde->she", key_h, after_bf, preferred_element_type=jnp.float32),
        0.0,
    )
    return (
        normed,
        grad_q.reshape(tokens, local_width).astype(jnp.bfloat16),
        grad_k.reshape(tokens, local_width).astype(jnp.bfloat16),
        grad_v.reshape(tokens, local_width).astype(jnp.bfloat16),
    )


def solution(mesh):
    in_specs = (
        P("seq", "head"),
        P("seq", "head"),
        P("seq", "head"),
        P("seq", "head"),
        P("head"),
        P("seq"),
    )
    out_specs = (P("seq", "head"), P("seq", "head"), P("seq", "head"), P("seq", "head"))
    return jax.shard_map(
        on_device, mesh=mesh, in_specs=in_specs, out_specs=out_specs, check_vma=False
    )
```

profile of v0, /device:TPU:1, one launch (start us, length us, event | category | flops | bytes accessed | tf_op | source)
XLA Modules:
  0.0 668.2 jit_solution(6544364691596696745)
XLA Ops:
  7.2 1.4 slice.3
  8.6 3.0 copy.64
  11.6 2.1 copy.37
  13.8 1.3 fusion.28
  15.1 1.4 fusion.7
  17.2 2.6 copy.60
  21.2 130.1 %all-reduce = f32[64]{0:T(128)S(1)} all-reduce(f32[64]{0:T(128)S(1)} %dynamic-update-slice), channel_id=1, replica_groups=mesh['seq'=64,'head'=4] {'seq'}, use_global_device_ids=true, to_apply=%add | all-reduce | flops 64 | bytes 512
  152.5 4.9 select_convert_fusion.1
  157.5 3.6 copy-done.1
  161.1 4.9 fusion.3
  166.0 2.5 while.26
  168.5 4.6 multiply_reduce_fusion.1
  173.2 3.5 copy.41
  176.7 2.8 multiply_reduce_fusion
  179.5 8.9 %all-reduce.1 = (f32[768]{0:T(1024)S(1)}, f32[768]{0:T(1024)S(1)}) all-reduce(f32[768]{0:T(1024)S(1)} %get-tuple-element.171, f32[768]{0:T(1024)S(1)} %multiply_reduce_fusion), channel_id=1, replica_groups=mesh['seq'=64,'head'=4] {'head'}, use_global_device_ids=true, to_apply=%region_4.5 | all-reduce | flops 1536 | bytes 12288 | tf_op jit(solution)/shard_map/psum | solution.py:73
  188.4 4.9 multiply_convert_fusion
  193.3 2.6 copy.61
  196.0 3.3 fusion.11
  199.3 4.2 select_convert_fusion
  203.6 7.4 %fusion.31 = f32[8,768,128]{1,2,0:T(8,128)} fusion(bf16[8,768,768]{2,1,0:T(8,128)(2,1)S(1)} %select_convert_fusion, bf16[768,8,128]{0,2,1:T(8,128)(2,1)} %copy-done.4), kind=kOutput, calls=%fused_computation.50 | convolution fusion | flops 1207959552 | bytes 14155776 | tf_op jit(solution)/shard_map/hts,shd->thd/dot_general | solution.py:95
  210.9 4.1 fusion.1
  215.0 2.7 copy.55
  217.7 7.4 %fusion.32 = f32[8,128,768]{2,1,0:T(8,128)} fusion(bf16[768,8,128]{0,2,1:T(8,128)(2,1)} %bitcast.96, bf16[8,768,768]{2,1,0:T(8,128)(2,1)} %copy-done.1), kind=kOutput, calls=%fused_computation.51 | convolution fusion | flops 1207959552 | bytes 14155776 | tf_op jit(solution)/shard_map/hts,the->she/dot_general | solution.py:107
  225.5 3.0 fusion.33
  228.6 264.2 %all-gather.7.cloned.1.call-done = f32[512,128,128]{2,1,0:T(8,128)} async-done(((f32[8,128,128]{2,1,0:T(8,128)}), f32[512,128,128]{2,1,0:T(8,128)}) %all-gather.7.cloned.1.call-update) | async-done | bytes 33554448 | tf_op jit(solution)/shard_map/all_gather | solution.py:16
  492.8 155.5 %while.27 = (s32[]{:T(128)}, f32[8,128,128]{2,1,0:T(8,128)S(1)}, s32[]{:T(128)}, f32[64,8,128,128]{3,2,1,0:T(8,128)}, f32[64]{0:T(128)S(1)}, /*index=5*/s32[]{:T(128)}, s32[]{:T(128)}, s32[]{:T(128)}, s32[]{:T(128)}, f32[1]{0:T(128)}) while((s32[]{:T(128)}, f32[8,128,128]{2,1,0:T(8,128)S(1)}, s32[]{:T(128)}, f32[64,8,128,128]{3,2,1,0:T(8,128)}, ...), condition=%wide.region_8.9_spmd, body=%wide.region_7.8_spmd.sunk | while | flops 262151 | bytes 1573051 | solution.py:25
  494.1 1.2 bitcast_add_fusion.8
  499.1 1.2 bitcast_add_fusion.8
  501.6 1.2 bitcast_add_fusion.8
  504.1 1.2 bitcast_add_fusion.8
  506.6 1.2 bitcast_add_fusion.8
  509.2 1.2 bitcast_add_fusion.8
  511.7 1.2 bitcast_add_fusion.8
  516.7 1.2 bitcast_add_fusion.8
  519.2 1.2 bitcast_add_fusion.8
  521.7 1.2 bitcast_add_fusion.8
  524.2 1.2 bitcast_add_fusion.8
  529.2 1.2 bitcast_add_fusion.8
  534.2 1.2 bitcast_add_fusion.8
  536.7 1.2 bitcast_add_fusion.8
  539.2 1.2 bitcast_add_fusion.8
  541.8 1.2 bitcast_add_fusion.8
  546.8 1.2 bitcast_add_fusion.8
  549.3 1.2 bitcast_add_fusion.8
  551.8 1.2 bitcast_add_fusion.8
  554.3 1.2 bitcast_add_fusion.8
  556.8 1.2 bitcast_add_fusion.8
  559.3 1.2 bitcast_add_fusion.8
  564.3 1.2 bitcast_add_fusion.8
  566.8 1.2 bitcast_add_fusion.8
  569.3 1.2 bitcast_add_fusion.8
  571.8 1.2 bitcast_add_fusion.8
  576.9 1.2 bitcast_add_fusion.8
  581.9 1.2 bitcast_add_fusion.8
  584.4 1.2 bitcast_add_fusion.8
  586.9 1.2 bitcast_add_fusion.8
  589.4 1.2 bitcast_add_fusion.8
  594.4 1.2 bitcast_add_fusion.8
  596.9 1.2 bitcast_add_fusion.8
  599.4 1.2 bitcast_add_fusion.8
  648.3 4.2 add_convert_fusion
  652.5 2.6 copy.57
  655.1 3.7 fusion
  658.8 2.6 copy.56
  (130 shorter events, 76.3 us)
Async XLA Ops:
  7.2 7.9 %copy-start = (bf16[768,1024]{1,0:T(8,128)(2,1)S(1)}, bf16[768,1024]{1,0:T(8,128)(2,1)}, u32[]{:S(2)}) copy-start(bf16[768,1024]{1,0:T(8,128)(2,1)} %param.12) | copy-start | bytes 4718596
  7.2 158.8 %all-gather.5.cloned.1.call-start = ((), (), s32[]{:S(2)}) async-start(), calls=%async_computation | async-start | bytes 34078720 | tf_op jit(solution)/shard_map/all_gather | solution.py:16
  11.6 2.1 copy-start.7
  13.7 2.7 copy-start.4
  16.5 476.3 %all-gather.7.cloned.1.call-start = ((), (), s32[]{:S(2)}) async-start(), calls=%async_computation.1 | async-start | bytes 34078720 | tf_op jit(solution)/shard_map/all_gather | solution.py:16
  17.2 2.6 copy-start.9
  151.7 0.8 copy-start.5
  157.4 3.6 copy-start.1
  173.2 3.5 copy-start.8
  196.0 3.3 copy-start.6
  203.6 7.4 %copy-start.2 = (bf16[8,768,768]{2,1,0:T(8,128)(2,1)}, bf16[8,768,768]{2,1,0:T(8,128)(2,1)S(1)}, u32[]{:S(2)}) copy-start(bf16[8,768,768]{2,1,0:T(8,128)(2,1)S(1)} %select_convert_fusion) | copy-start | bytes 28311556
  215.0 10.1 %slice-start = ((s8[9437184]{0:T(1024)(128)(4,1)}), s8[1048576]{0:T(1024)(128)(4,1)S(1)}, s32[]{:S(2)}) async-start(s8[9437184]{0:T(1024)(128)(4,1)} %bitcast.91), calls=%async_computation.2 | async-start | bytes 2097152
  217.7 7.4 %slice-start.1 = ((s8[9437184]{0:T(1024)(128)(4,1)}), s8[4194304]{0:T(1024)(128)(4,1)S(1)}, s32[]{:S(2)}) async-start(s8[9437184]{0:T(1024)(128)(4,1)} %bitcast.91), calls=%async_computation.3 | async-start | bytes 8388608
  217.7 7.4 %slice-start.2 = ((s8[9437184]{0:T(1024)(128)(4,1)}), s8[4194304]{0:T(1024)(128)(4,1)S(1)}, s32[]{:S(2)}) async-start(s8[9437184]{0:T(1024)(128)(4,1)} %bitcast.91), calls=%async_computation.4 | async-start | bytes 8388608
  217.7 7.8 %copy-start.3 = (bf16[768,1024]{0,1:T(8,128)(2,1)S(1)}, bf16[768,1024]{0,1:T(8,128)(2,1)}, u32[]{:S(2)}) copy-start(bf16[768,1024]{0,1:T(8,128)(2,1)} %copy.60) | copy-start | bytes 4718596
Sparse Core Ops, SparseCore 0:
  16.6 147.0 all-gather.4
  199.4 293.3 all-gather.6
where the time goes:
time: 673 us; the launch traced here: 668 us
  waiting for transfers between devices  264 us (39%)
  blocking collectives  139 us (21%)
  other arithmetic  87.9 us (13%)
  local copies, waits for them, and re-layouts  66.4 us (10%)
  matrix products  53.2 us (8%)
  loops' own time  42.5 us (6%)
  between operations  14.9 us (2%)
    all_gather x2, waiting for transfers between devices, prefix(): gathered = jax.tree.map(lambda a: lax.all_gather(a, axis), part)  264 us
    unnamed x1, blocking collectives  130 us
    add x63, other arithmetic, combine(): late_state + (1.0 - late_flag) * early_state  78.5 us
    another operation x2, loops' own time, prefix(): return lax.fori_loop(0, ahead, one, state)  42.5 us
    dynamic_slice x63, local copies, waits for them, and re-layouts, one(): lax.dynamic_index_in_dim(a, source, 0, False)  37 us
    unnamed x33, local copies, waits for them, and re-layouts  17.1 us
  transfers between devices with their start and end apart: 2, of which 1 were waited for; matrix products, arithmetic and copies ran while one was open for 6% of the time, Pallas kernels for 0%

commit v1 on v0

v1 whole, which is shorter than its diff:
```python
import functools

import jax
import jax.numpy as jnp
from jax import lax
from jax.experimental import pallas as pl
from jax.experimental.pallas import tpu as pltpu
from jax.sharding import PartitionSpec as P

HEAD_DIM = 128
UNIT = 256
SLICE = 16
epsilon = 1e-06

F32 = jnp.float32
BF16 = jnp.bfloat16


def dot(left, right, contract):
    return lax.dot_general(
        left, right, ((contract[0:1], contract[1:2]), ((), ())), preferred_element_type=F32
    )


def unit(index):
    return slice(index * UNIT, (index + 1) * UNIT)


def columns(index):
    return slice(index * HEAD_DIM, (index + 1) * HEAD_DIM)


def causal():
    rows = lax.broadcasted_iota(jnp.int32, (UNIT, UNIT), 0)
    return rows >= lax.broadcasted_iota(jnp.int32, (UNIT, UNIT), 1)


def tile_mask(doc_ref, later, earlier):
    if later == earlier:
        return causal()
    return jnp.full((UNIT, UNIT), doc_ref[later * UNIT] == doc_ref[earlier * UNIT])


def masked_rows(keep, rows):
    return jnp.where(jnp.full(rows.shape, keep), rows, jnp.zeros_like(rows))


def column_of(row):
    return jnp.transpose(jnp.broadcast_to(row, (HEAD_DIM, row.shape[1])))


def tail_kernel(heads, doc_ref, key_ref, value_ref, state_ref):
    tokens = key_ref.shape[0]
    units = tokens // UNIT
    last = doc_ref[tokens - 1]
    parts = HEAD_DIM // SLICE
    for h in range(heads):
        total = jnp.zeros((HEAD_DIM, HEAD_DIM), F32)
        for u in range(units):
            key = masked_rows(doc_ref[u * UNIT] == last, key_ref[unit(u), columns(h)])
            total += dot(key, value_ref[unit(u), columns(h)], (0, 0))
        state_ref[h * parts : (h + 1) * parts, 0:SLICE, :] = total.reshape(parts, SLICE, HEAD_DIM)
    offset = lax.axis_index("seq") * tokens
    flag = jnp.where(last >= offset, 0.0, 1.0).astype(F32)
    state_ref[:, SLICE:, :] = jnp.full((state_ref.shape[0], 8, HEAD_DIM), flag)


def scan_kernel(reverse, part_ref, flag_ref, state_ref):
    count = part_ref.shape[0]
    carry = jnp.zeros((SLICE, HEAD_DIM), F32)
    for step in range(count):
        b = count - 1 - step if reverse else step
        state_ref[b] = carry
        carry = part_ref[b, 0:SLICE, :] + flag_ref[b, 0:1, :] * carry


def local_kernel(heads, doc_ref, query_ref, key_ref, value_ref, out_ref):
    units = query_ref.shape[0] // UNIT
    for h in range(heads):
        for t in range(units):
            total = jnp.zeros((UNIT, HEAD_DIM), F32)
            for s in range(t + 1):
                score = dot(query_ref[unit(t), columns(h)], key_ref[unit(s), columns(h)], (1, 1))
                score = jnp.where(tile_mask(doc_ref, t, s), score, 0.0).astype(BF16)
                total += dot(score, value_ref[unit(s), columns(h)], (1, 0))
            out_ref[unit(t), columns(h)] = total


def attended_kernel(heads, doc_ref, query_ref, local_ref, cotangent_ref, gain_ref, prefix_ref,
                    out_ref, sums_ref, square, cross):
    tokens = query_ref.shape[0]
    offset = lax.axis_index("seq") * tokens
    step = pl.program_id(0)

    @pl.when(step == 0)
    def _():
        square[...] = jnp.zeros_like(square)
        cross[...] = jnp.zeros_like(cross)

    for u in range(tokens // UNIT):
        squares = square[unit(u), :]
        crosses = cross[unit(u), :]
        for h in range(heads):
            query = masked_rows(doc_ref[u * UNIT] < offset, query_ref[unit(u), columns(h)])
            prefix = prefix_ref[h * HEAD_DIM : (h + 1) * HEAD_DIM, :].astype(BF16)
            out = local_ref[unit(u), columns(h)] + dot(query, prefix, (1, 0))
            out_ref[unit(u), columns(h)] = out
            scaled = gain_ref[0:1, columns(h)] * cotangent_ref[unit(u), columns(h)].astype(F32)
            squares += out * out
            crosses += scaled * out
        square[unit(u), :] = squares
        cross[unit(u), :] = crosses

    @pl.when(step == pl.num_programs(0) - 1)
    def _():
        sums_ref[0:1, :] = jnp.sum(jnp.transpose(square[...]), axis=0, keepdims=True)
        sums_ref[1:2, :] = jnp.sum(jnp.transpose(cross[...]), axis=0, keepdims=True)


def norm_kernel(heads, features, doc_ref, sums_ref, out_ref, query_ref, cotangent_ref, gain_ref,
                normed_ref, grad_ref, state_ref, inverse, factor):
    tokens = query_ref.shape[0]
    offset = lax.axis_index("seq") * tokens

    @pl.when(pl.program_id(0) == 0)
    def _():
        sums = sums_ref[0] + sums_ref[1] + sums_ref[2] + sums_ref[3]
        inv = lax.rsqrt(sums[0:1] / features + epsilon)
        inverse[...] = column_of(inv)
        factor[...] = column_of(inv * inv * sums[1:2] / features)

    parts = HEAD_DIM // SLICE
    for h in range(heads):
        total = jnp.zeros((HEAD_DIM, HEAD_DIM), F32)
        for u in range(tokens // UNIT):
            out = out_ref[unit(u), columns(h)]
            gain = gain_ref[0:1, columns(h)]
            inv = inverse[unit(u), :]
            normed_ref[unit(u), columns(h)] = (out * inv * gain).astype(BF16)
            scaled = gain * cotangent_ref[unit(u), columns(h)].astype(F32)
            grad = (inv * (scaled - out * factor[unit(u), :])).astype(BF16)
            grad_ref[unit(u), columns(h)] = grad
            query = masked_rows(doc_ref[u * UNIT] < offset, query_ref[unit(u), columns(h)])
            total += dot(query, grad, (0, 0))
        state_ref[h * parts : (h + 1) * parts] = total.reshape(parts, SLICE, HEAD_DIM)


def back_kernel(heads, doc_ref, query_ref, key_ref, value_ref, grad_ref, prefix_ref,
                grad_q_ref, key_part_ref, value_part_ref):
    tokens = query_ref.shape[0]
    units = tokens // UNIT
    offset = lax.axis_index("seq") * tokens
    for h in range(heads):
        prefix = prefix_ref[h * HEAD_DIM : (h + 1) * HEAD_DIM, :].astype(BF16)
        grad_k = [jnp.zeros((UNIT, HEAD_DIM), F32) for _ in range(units)]
        grad_v = [jnp.zeros((UNIT, HEAD_DIM), F32) for _ in range(units)]
        for t in range(units):
            query = query_ref[unit(t), columns(h)]
            grad = grad_ref[unit(t), columns(h)]
            grad_q = dot(masked_rows(doc_ref[t * UNIT] < offset, grad), prefix, (1, 1))
            for s in range(t + 1):
                key = key_ref[unit(s), columns(h)]
                mask = tile_mask(doc_ref, t, s)
                score = jnp.where(mask, dot(query, key, (1, 1)), 0.0).astype(BF16)
                back = dot(grad, value_ref[unit(s), columns(h)], (1, 1))
                back = jnp.where(mask, back, 0.0).astype(BF16)
                grad_q += dot(back, key, (1, 0))
                grad_k[s] += dot(back, query, (0, 0))
                grad_v[s] += dot(score, grad, (0, 0))
            grad_q_ref[unit(t), columns(h)] = grad_q.astype(BF16)
        for s in range(units):
            key_part_ref[unit(s), columns(h)] = grad_k[s]
            value_part_ref[unit(s), columns(h)] = grad_v[s]


def finish_kernel(heads, doc_ref, key_ref, value_ref, key_part_ref, value_part_ref, suffix_ref,
                  grad_k_ref, grad_v_ref):
    tokens = key_ref.shape[0]
    last = doc_ref[tokens - 1]
    for h in range(heads):
        suffix = suffix_ref[h * HEAD_DIM : (h + 1) * HEAD_DIM, :].astype(BF16)
        for u in range(tokens // UNIT):
            closing = doc_ref[u * UNIT] == last
            value = masked_rows(closing, value_ref[unit(u), columns(h)])
            grad_k = key_part_ref[unit(u), columns(h)] + dot(value, suffix, (1, 1))
            grad_k_ref[unit(u), columns(h)] = grad_k.astype(BF16)
            key = masked_rows(closing, key_ref[unit(u), columns(h)])
            grad_v = value_part_ref[unit(u), columns(h)] + dot(key, suffix, (1, 0))
            grad_v_ref[unit(u), columns(h)] = grad_v.astype(BF16)


def on_device(queries, keys, values, cotangent, norm_gain, doc_start):
    tokens, width = queries.shape
    blocks = lax.axis_size("seq")
    heads = width // HEAD_DIM
    per_step = 2
    steps = heads // per_step
    parts = HEAD_DIM // SLICE
    features = width * lax.axis_size("head")
    gain = norm_gain.reshape(1, width)

    docs = pl.BlockSpec(memory_space=pltpu.SMEM)
    wide = pl.BlockSpec((tokens, per_step * HEAD_DIM), lambda i: (0, i))
    gains = pl.BlockSpec((1, per_step * HEAD_DIM), lambda i: (0, i))
    states = pl.BlockSpec((per_step * HEAD_DIM, HEAD_DIM), lambda i: (i, 0))
    tall = jax.ShapeDtypeStruct((tokens, width), F32)
    narrow = jax.ShapeDtypeStruct((tokens, width), BF16)

    def cost(products, arrays):
        return pl.CostEstimate(
            flops=2 * products * tokens * width, bytes_accessed=arrays * tokens * width, transcendentals=0
        )

    def call(kernel, ins, outs, shapes, estimate, scratch=()):
        return pl.pallas_call(
            kernel,
            grid=(steps,),
            in_specs=ins,
            out_specs=outs,
            out_shape=shapes,
            scratch_shapes=list(scratch),
            cost_estimate=estimate,
            compiler_params=pltpu.CompilerParams(vmem_limit_bytes=40 * 1024 * 1024),
        )

    tail = call(
        functools.partial(tail_kernel, per_step),
        [docs, wide, wide],
        pl.BlockSpec((per_step * parts, SLICE + 8, HEAD_DIM), lambda i: (i, 0, 0)),
        jax.ShapeDtypeStruct((blocks, SLICE + 8, HEAD_DIM), F32),
        cost(HEAD_DIM, 5),
    )(doc_start, keys, values)

    def exchange(data):
        return lax.all_to_all(data, "seq", 0, 0)

    def scan(part, flags, reverse):
        return pl.pallas_call(
            functools.partial(scan_kernel, reverse),
            out_shape=jax.ShapeDtypeStruct((blocks, SLICE, HEAD_DIM), F32),
        )(part, flags)

    tails = exchange(tail)
    flags = tails[:, SLICE:, :]
    prefix = exchange(scan(tails, flags, False)).reshape(heads * HEAD_DIM, HEAD_DIM)

    local = call(
        functools.partial(local_kernel, per_step),
        [docs, wide, wide, wide],
        wide,
        tall,
        cost(2 * 512, 10),
    )(doc_start, queries, keys, values)

    partial_rows = pltpu.VMEM((tokens, HEAD_DIM), F32)
    attended, sums = call(
        functools.partial(attended_kernel, per_step),
        [docs, wide, wide, wide, gains, states],
        [wide, pl.BlockSpec((2, tokens), lambda i: (0, 0))],
        [tall, jax.ShapeDtypeStruct((2, tokens), F32)],
        cost(HEAD_DIM, 12),
        [partial_rows, partial_rows],
    )(doc_start, queries, local, cotangent, gain, prefix)

    count = lax.axis_size("head")
    all_sums = jnp.stack(
        [sums]
        + [
            lax.ppermute(sums, "head", [(i, (i + step) % count) for i in range(count)])
            for step in range(1, count)
        ]
    )
    normed, grad_out, head_state = call(
        functools.partial(norm_kernel, per_step, features),
        [docs, pl.BlockSpec((count, 2, tokens), lambda i: (0, 0, 0)), wide, wide, wide, gains],
        [wide, wide, pl.BlockSpec((per_step * parts, SLICE, HEAD_DIM), lambda i: (i, 0, 0))],
        [narrow, narrow, jax.ShapeDtypeStruct((blocks, SLICE, HEAD_DIM), F32)],
        cost(HEAD_DIM, 13),
        [partial_rows, partial_rows],
    )(doc_start, all_sums, attended, queries, cotangent, gain)

    suffix = exchange(scan(exchange(head_state), flags, True)).reshape(heads * HEAD_DIM, HEAD_DIM)

    grad_q, key_part, value_part = call(
        functools.partial(back_kernel, per_step),
        [docs, wide, wide, wide, wide, states],
        [wide, wide, wide],
        [narrow, tall, tall],
        cost(5 * 512, 18),
    )(doc_start, queries, keys, values, grad_out, prefix)

    grad_k, grad_v = call(
        functools.partial(finish_kernel, per_step),
        [docs, wide, wide, wide, wide, states],
        [wide, wide],
        [narrow, narrow],
        cost(2 * HEAD_DIM, 16),
    )(doc_start, keys, values, key_part, value_part, suffix)
    return normed, grad_q, grad_k, grad_v


def solution(mesh):
    wide = P("seq", "head")
    return jax.shard_map(
        on_device,
        mesh=mesh,
        in_specs=(wide, wide, wide, wide, P("head"), P("seq")),
        out_specs=(wide, wide, wide, wide),
        check_vma=False,
    )
```

time: 673 us -> 156 us (0.23)
  waiting for transfers between devices: 264 us -> 9.89 us
  other arithmetic: 87.9 us -> 0.01 us
  blocking collectives: 139 us -> 61.1 us
  matrix products: 53.2 us -> 0 us
  Pallas kernels: 0 us -> 42.6 us
  local copies, waits for them, and re-layouts: 66.4 us -> 23.9 us
  loops' own time: 42.5 us -> 0 us
  starting transfers between devices: 0.08 us -> 16.7 us
  between operations: 14.9 us -> 0.77 us
    all_gather x2 -> x0, waiting for transfers between devices: 264 us -> none  [prefix(): gathered = jax.tree.map(lambda a: lax.all_gather(a, axis), part)]
    unnamed x1 -> x0, blocking collectives: 130 us -> none
    add x63 -> x0, other arithmetic: 78.5 us -> none  [combine(): late_state + (1.0 - late_flag) * early_state]
    all_to_all x0 -> x2, blocking collectives: none -> 61.1 us  [exchange(): return lax.all_to_all(data, 'seq', 0, 0)]
    dot_general x12 -> x0, matrix products: 53.2 us -> none  [the longest x1 7.43 us: on_device(): jnp.einsum('hts,the->she', attend, grad_out, preferred_element_type=jnp.f...]
    pallas_call x0 -> x8, Pallas kernels: none -> 42.6 us  [the longest x1 16.1 us: on_device(): call(functools.partial(back_kernel, per_step), [docs, wide, wide, wide, w...]
    another operation x2 -> x0, loops' own time: 42.5 us -> none  [prefix(): return lax.fori_loop(0, ahead, one, state)]
    dynamic_slice x63 -> x0, local copies, waits for them, and re-layouts: 37 us -> none  [one(): lax.dynamic_index_in_dim(a, source, 0, False)]
  transfers between devices with their start and end apart: 2 -> 5, of which waited for: 1 -> 3; matrix products, arithmetic and copies ran while one was open for 6% -> 0% of each run, Pallas kernels for 0% -> 15%
where the time goes in v1:
time: 156 us; the launch traced here: 155 us
  blocking collectives  61.1 us (39%)
  Pallas kernels  42.6 us (27%)
  local copies, waits for them, and re-layouts  23.9 us (15%)
  starting transfers between devices  16.7 us (11%)
  waiting for transfers between devices  9.89 us (6%)
    all_to_all x2, blocking collectives, exchange(): return lax.all_to_all(data, 'seq', 0, 0)  61.1 us
    unnamed x42, local copies, waits for them, and re-layouts  23.2 us
    pallas_call x1, Pallas kernels, on_device(): call(functools.partial(back_kernel, per_step), [docs, wide, wide, wide, w...  16.1 us
    all_to_all x2, starting transfers between devices, exchange(): return lax.all_to_all(data, 'seq', 0, 0)  12.9 us
    pallas_call x1, Pallas kernels, on_device(): call(functools.partial(local_kernel, per_step), [docs, wide, wide, wide],...  7.27 us
    all_to_all x2, waiting for transfers between devices, exchange(): return lax.all_to_all(data, 'seq', 0, 0)  6.88 us
    pallas_call x1, Pallas kernels, on_device(): call(functools.partial(finish_kernel, per_step), [docs, wide, wide, wide,...  4.76 us
    pallas_call x2, Pallas kernels, scan(): pl.pallas_call(functools.partial(scan_kernel, reverse), out_shape=jax.Sha...  4.15 us
  transfers between devices with their start and end apart: 5, of which 3 were waited for; matrix products, arithmetic and copies ran while one was open for 0% of the time, Pallas kernels for 15%

profile of v1, /device:TPU:1, one launch (start us, length us, event | category | flops | bytes accessed | tf_op | source)
XLA Modules:
  0.0 155.0 jit_solution(5325535846393974817)
XLA Ops:
  0.6 0.0 copy-start
  0.6 1.4 copy-done
  2.0 0.0 copy-start.2
  2.0 1.4 copy-done.2
  3.4 0.0 copy-start.15
  3.5 0.7 copy-done.15
  4.1 2.2 %shard_map.94 = f32[64,24,128]{2,1,0:T(8,128)S(1)} custom-call(s32[768]{0:T(1024)S(1)} %copy-done.15, bf16[768,1024]{1,0:T(8,128)(2,1)S(1)} %copy-done, bf16[768,1024]{1,0:T(8,128)(2,1)S(1)} %copy-done.2), custom_call_target="tpu_custom_call" | custom-call | flops 201326592 | bytes 3932160 | tf_op jit(solution)/shard_map/pallas_call | solution.py:226
  6.4 0.0 copy-start.3
  6.4 35.9 %all_to_all.20.part_ref = f32[64,24,128]{2,1,0:T(8,128)S(1)} all-to-all(f32[64,24,128]{2,1,0:T(8,128)S(1)} %shard_map.94), channel_id=1, replica_groups=mesh['seq'=64,'head'=4] {'seq'}, dimensions={0} | all-to-all | bytes 1572864 | tf_op jit(solution)/shard_map/all_to_all | solution.py:235
  42.3 0.0 copy-start.20
  42.3 0.9 copy-done.20
  43.2 0.0 copy-start.1
  43.2 0.0 copy-start.16
  43.2 0.7 slice.4.flag_ref
  43.9 2.1 %shard_map.95 = f32[64,16,128]{2,1,0:T(8,128)} custom-call(f32[64,24,128]{2,1,0:T(8,128)} %copy-done.20, f32[64,8,128]{2,1,0:T(8,128)} %slice.4.flag_ref), custom_call_target="tpu_custom_call" | custom-call | tf_op jit(solution)/shard_map/pallas_call | solution.py:238
  46.0 6.4 %all-to-all-start.1 = ((f32[64,16,128]{2,1,0:T(8,128)}), f32[64,16,128]{2,1,0:T(8,128)}, u32[]{:S(2)}, u32[]{:S(2)}) async-start(f32[64,16,128]{2,1,0:T(8,128)} %shard_map.95), calls=%async_computation.1 | async-start | bytes 1048576 | tf_op jit(solution)/shard_map/all_to_all | solution.py:235
  52.4 0.0 copy-done.3
  52.4 0.0 copy-done.1
  52.4 0.0 copy-done.16
  52.4 0.0 copy-start.4
  52.4 1.4 copy-done.4
  53.8 0.0 copy-start.17
  53.8 7.3 %shard_map.93.local_ref = f32[768,1024]{1,0:T(8,128)S(1)} custom-call(s32[768]{0:T(1024)S(1)} %copy-done.16, bf16[768,1024]{1,0:T(8,128)(2,1)S(1)} %copy-done.4, bf16[768,1024]{1,0:T(8,128)(2,1)S(1)} %copy-done.1, bf16[768,1024]{1,0:T(8,128)(2,1)S(1)} %copy-done.3), custom_call_target="tpu_custom_call" | custom-call | flops 1610612736 | bytes 7864320 | tf_op jit(solution)/shard_map/pallas_call | solution.py:247
  61.1 0.0 copy-start.7
  61.1 1.6 %copy-done.7 = f32[768,1024]{1,0:T(8,128)} copy-done((f32[768,1024]{1,0:T(8,128)}, f32[768,1024]{1,0:T(8,128)S(1)}, u32[]{:S(2)}) %copy-start.7) | copy-done | bytes 3145752
  62.8 6.9 %all-to-all-done.1 = f32[64,16,128]{2,1,0:T(8,128)} async-done(((f32[64,16,128]{2,1,0:T(8,128)}), f32[64,16,128]{2,1,0:T(8,128)}, u32[]{:S(2)}, u32[]{:S(2)}) %all-to-all-start.1) | async-done | bytes 524320 | tf_op jit(solution)/shard_map/all_to_all | solution.py:235
  69.6 0.0 copy-done.17
  69.6 0.0 copy-start.5
  69.6 1.4 copy-done.5
  71.0 0.0 copy-start.8
  71.0 1.9 %copy-done.8 = f32[768,1024]{1,0:T(8,128)S(1)} copy-done((f32[768,1024]{1,0:T(8,128)S(1)}, f32[768,1024]{1,0:T(8,128)}, u32[]{:S(2)}) %copy-start.8) | copy-done | bytes 3145752
  72.9 0.0 copy-start.9
  72.9 1.4 copy-done.9
  74.3 0.0 copy-start.10
  74.3 4.0 %shard_map.96 = (f32[768,1024]{1,0:T(8,128)S(1)}, f32[2,768]{1,0:T(2,128)S(1)}) custom-call(s32[768]{0:T(1024)S(1)} %copy-done.16, bf16[768,1024]{1,0:T(8,128)(2,1)S(1)} %copy-done.5, f32[768,1024]{1,0:T(8,128)S(1)} %copy-done.8, bf16[768,1024]{1,0:T(8,128)(2,1)S(1)} %copy-done.9, f32[1,1024]{1,0:T(1,128)S(1)} %bitcast.7, f32[1024,128]{1,0:T(8,128)} %bitcast.1.prefix_ref), custom_call_target="tpu_custom_call" | custom-call | flops 201326592 | bytes 9437184 | tf_op jit(solution)/shard_map/pallas_call | solution.py:256
  78.3 2.8 %collective-permute-start.2 = (f32[2,768]{1,0:T(2,128)S(1)}, f32[2,768]{1,0:T(2,128)S(1)}, u32[]{:S(2)}, u32[]{:S(2)}) collective-permute-start(f32[2,768]{1,0:T(2,128)S(1)} %get-tuple-element.14), channel_id=1, source_target_pairs={{0,3},{1,0},{2,1},{3,2},{4,7},{5,4},{6,5},{7,6},{8,11},{9,8},{10,9... | collective-permute-start | bytes 18440 | tf_op jit(solution)/shard_map/ppermute | solution.py:269
  81.1 0.3 collective-permute-start.1
  81.5 0.7 collective-permute-start
  82.2 0.0 collective-permute-done.2
  82.2 2.9 %collective-permute-done.1 = f32[2,768]{1,0:T(2,128)S(1)} collective-permute-done((f32[2,768]{1,0:T(2,128)S(1)}, f32[2,768]{1,0:T(2,128)S(1)}, u32[]{:S(2)}, u32[]{:S(2)}) %collective-permute-start.1) | collective-permute-done | bytes 6176 | tf_op jit(solution)/shard_map/ppermute | solution.py:269
  85.1 0.1 collective-permute-done
  85.2 0.0 copy-done.10
  85.2 4.1 %shard_map.97 = (bf16[768,1024]{1,0:T(8,128)(2,1)}, bf16[768,1024]{1,0:T(8,128)(2,1)S(1)}, f32[64,16,128]{2,1,0:T(8,128)S(1)}) custom-call(s32[768]{0:T(1024)S(1)} %copy-done.16, f32[4,2,768]{2,1,0:T(2,128)S(1)} %pad_maximum_fusion.sums_ref, f32[768,1024]{1,0:T(8,128)S(1)} %get-tuple-element.15.out_ref, bf16[768,1024]{1,0:T(8,128)(2,1)S(1)} %copy-done.5, ...), custom_call_target="tpu_custom_call" | custom-call | flops 201326592 | bytes 10223616 | tf_op jit(solution)/shard_map/pallas_call | solution.py:273
  89.3 0.0 copy-start.18
  89.3 1.1 copy-done.18
  90.5 25.2 %all_to_all.21.part_ref = f32[64,16,128]{2,1,0:T(8,128)} all-to-all(f32[64,16,128]{2,1,0:T(8,128)S(1)} %get-tuple-element.21), channel_id=1, replica_groups=mesh['seq'=64,'head'=4] {'seq'}, dimensions={0} | all-to-all | bytes 1048576 | tf_op jit(solution)/shard_map/all_to_all | solution.py:235
  115.6 2.0 %shard_map.99 = f32[64,16,128]{2,1,0:T(8,128)} custom-call(f32[64,16,128]{2,1,0:T(8,128)} %all_to_all.21.part_ref, f32[64,8,128]{2,1,0:T(8,128)} %slice.4.flag_ref), custom_call_target="tpu_custom_call" | custom-call | tf_op jit(solution)/shard_map/pallas_call | solution.py:238
  117.7 6.5 %all-to-all-start.3 = ((f32[64,16,128]{2,1,0:T(8,128)}), f32[64,16,128]{2,1,0:T(8,128)}, u32[]{:S(2)}, u32[]{:S(2)}) async-start(f32[64,16,128]{2,1,0:T(8,128)} %shard_map.99), calls=%async_computation.3 | async-start | bytes 1048576 | tf_op jit(solution)/shard_map/all_to_all | solution.py:235
  124.2 0.0 copy-start.6
  124.2 1.4 copy-done.6
  125.6 0.0 copy-start.19
  125.6 1.4 copy-done.19
  127.0 16.1 %shard_map.98 = (bf16[768,1024]{1,0:T(8,128)(2,1)}, f32[768,1024]{1,0:T(8,128)S(1)}, f32[768,1024]{1,0:T(8,128)S(1)}) custom-call(s32[768]{0:T(1024)S(1)} %copy-done.16, bf16[768,1024]{1,0:T(8,128)(2,1)S(1)} %copy-done.6, bf16[768,1024]{1,0:T(8,128)(2,1)S(1)} %copy-done.1, bf16[768,1024]{1,0:T(8,128)(2,1)S(1)} %copy-done.3, ...), custom_call_target="tpu_custom_call" | custom-call | flops 4026531840 | bytes 14155776 | tf_op jit(solution)/shard_map/pallas_call | solution.py:284
  143.1 0.0 copy-start.11
  143.1 1.6 %copy-done.11 = f32[768,1024]{1,0:T(8,128)} copy-done((f32[768,1024]{1,0:T(8,128)}, f32[768,1024]{1,0:T(8,128)S(1)}, u32[]{:S(2)}) %copy-start.11) | copy-done | bytes 3145752
  144.8 0.0 copy-start.13
  144.8 1.7 %copy-done.13 = f32[768,1024]{1,0:T(8,128)} copy-done((f32[768,1024]{1,0:T(8,128)}, f32[768,1024]{1,0:T(8,128)S(1)}, u32[]{:S(2)}) %copy-start.13) | copy-done | bytes 3145752
  146.5 0.0 all-to-all-done.3
  146.5 0.0 copy-start.12
  146.5 1.9 %copy-done.12 = f32[768,1024]{1,0:T(8,128)S(1)} copy-done((f32[768,1024]{1,0:T(8,128)S(1)}, f32[768,1024]{1,0:T(8,128)}, u32[]{:S(2)}) %copy-start.12) | copy-done | bytes 3145752
  148.3 0.0 copy-start.14
  148.4 1.9 %copy-done.14 = f32[768,1024]{1,0:T(8,128)S(1)} copy-done((f32[768,1024]{1,0:T(8,128)S(1)}, f32[768,1024]{1,0:T(8,128)}, u32[]{:S(2)}) %copy-start.14) | copy-done | bytes 3145752
  150.2 4.8 %shard_map.100 = (bf16[768,1024]{1,0:T(8,128)(2,1)}, bf16[768,1024]{1,0:T(8,128)(2,1)}) custom-call(s32[768]{0:T(1024)S(1)} %copy-done.16, bf16[768,1024]{1,0:T(8,128)(2,1)S(1)} %copy-done.1, bf16[768,1024]{1,0:T(8,128)(2,1)S(1)} %copy-done.3, f32[768,1024]{1,0:T(8,128)S(1)} %copy-done.12, f32[768,1024]{1,0:T(8,128)S(1)} %copy-done.14, ...), custom_call_target="tpu_custom_call" | custom-call | flops 402653184 | bytes 12582912 | tf_op jit(solution)/shard_map/pallas_call | solution.py:292
  (1 shorter events, 0.0 us)
Async XLA Ops:
  0.6 1.4 copy-start
  2.0 1.4 copy-start.2
  3.4 0.7 copy-start.15
  6.4 46.0 %copy-start.3 = (bf16[768,1024]{1,0:T(8,128)(2,1)S(1)}, bf16[768,1024]{1,0:T(8,128)(2,1)}, u32[]{:S(2)}) copy-start(bf16[768,1024]{1,0:T(8,128)(2,1)} %value_ref.7) | copy-start | bytes 4718596
  42.3 0.9 copy-start.20
  43.2 9.2 %copy-start.1 = (bf16[768,1024]{1,0:T(8,128)(2,1)S(1)}, bf16[768,1024]{1,0:T(8,128)(2,1)}, u32[]{:S(2)}) copy-start(bf16[768,1024]{1,0:T(8,128)(2,1)} %key_ref.7) | copy-start | bytes 4718596
  43.2 9.2 %copy-start.16 = (s32[768]{0:T(1024)S(1)}, s32[768]{0:T(1024)}, u32[]{:S(2)}) copy-start(s32[768]{0:T(1024)} %doc_ref.11) | copy-start | bytes 9220
  46.0 23.6 %all-to-all-start.1 = ((f32[64,16,128]{2,1,0:T(8,128)}), f32[64,16,128]{2,1,0:T(8,128)}, u32[]{:S(2)}, u32[]{:S(2)}) async-start(f32[64,16,128]{2,1,0:T(8,128)} %shard_map.95), calls=%async_computation.1 | async-start | bytes 1048576 | tf_op jit(solution)/shard_map/all_to_all | solution.py:235
  52.4 1.4 copy-start.4
  53.8 15.8 %copy-start.17 = (f32[1024]{0:T(1024)S(1)}, f32[1024]{0:T(1024)}, u32[]{:S(2)}) copy-start(f32[1024]{0:T(1024)} %param.10) | copy-start | bytes 12292
  61.1 1.6 %copy-start.7 = (f32[768,1024]{1,0:T(8,128)}, f32[768,1024]{1,0:T(8,128)S(1)}, u32[]{:S(2)}) copy-start(f32[768,1024]{1,0:T(8,128)S(1)} %shard_map.93.local_ref) | copy-start | bytes 9437188
  69.6 1.4 copy-start.5
  71.0 1.9 %copy-start.8 = (f32[768,1024]{1,0:T(8,128)S(1)}, f32[768,1024]{1,0:T(8,128)}, u32[]{:S(2)}) copy-start(f32[768,1024]{1,0:T(8,128)} %copy-done.7) | copy-start | bytes 9437188
  72.9 1.4 copy-start.9
  74.3 10.9 %copy-start.10 = (bf16[768,1024]{1,0:T(8,128)(2,1)S(1)}, bf16[768,1024]{1,0:T(8,128)(2,1)}, u32[]{:S(2)}) copy-start(bf16[768,1024]{1,0:T(8,128)(2,1)} %cotangent_ref.3) | copy-start | bytes 4718596
  78.3 3.9 %collective-permute-start.2 = (f32[2,768]{1,0:T(2,128)S(1)}, f32[2,768]{1,0:T(2,128)S(1)}, u32[]{:S(2)}, u32[]{:S(2)}) collective-permute-start(f32[2,768]{1,0:T(2,128)S(1)} %get-tuple-element.14), channel_id=1, source_target_pairs={{0,3},{1,0},{2,1},{3,2},{4,7},{5,4},{6,5},{7,6},{8,11},{9,8},{10,9... | collective-permute-start | bytes 18440 | tf_op jit(solution)/shard_map/ppermute | solution.py:269
  81.1 4.0 %collective-permute-start.1 = (f32[2,768]{1,0:T(2,128)S(1)}, f32[2,768]{1,0:T(2,128)S(1)}, u32[]{:S(2)}, u32[]{:S(2)}) collective-permute-start(f32[2,768]{1,0:T(2,128)S(1)} %get-tuple-element.14), channel_id=1, source_target_pairs={{0,2},{1,3},{2,0},{3,1},{4,6},{5,7},{6,4},{7,5},{8,10},{9,11},{10,... | collective-permute-start | bytes 18440 | tf_op jit(solution)/shard_map/ppermute | solution.py:269
  81.5 3.7 %collective-permute-start = (f32[2,768]{1,0:T(2,128)S(1)}, f32[2,768]{1,0:T(2,128)S(1)}, u32[]{:S(2)}, u32[]{:S(2)}) collective-permute-start(f32[2,768]{1,0:T(2,128)S(1)} %get-tuple-element.14), channel_id=1, source_target_pairs={{0,1},{1,2},{2,3},{3,0},{4,5},{5,6},{6,7},{7,4},{8,9},{9,10},{10,1... | collective-permute-start | bytes 18440 | tf_op jit(solution)/shard_map/ppermute | solution.py:269
  89.3 1.1 copy-start.18
  117.7 28.8 %all-to-all-start.3 = ((f32[64,16,128]{2,1,0:T(8,128)}), f32[64,16,128]{2,1,0:T(8,128)}, u32[]{:S(2)}, u32[]{:S(2)}) async-start(f32[64,16,128]{2,1,0:T(8,128)} %shard_map.99), calls=%async_computation.3 | async-start | bytes 1048576 | tf_op jit(solution)/shard_map/all_to_all | solution.py:235
  124.2 1.4 copy-start.6
  125.6 1.4 copy-start.19
  143.1 1.6 %copy-start.11 = (f32[768,1024]{1,0:T(8,128)}, f32[768,1024]{1,0:T(8,128)S(1)}, u32[]{:S(2)}) copy-start(f32[768,1024]{1,0:T(8,128)S(1)} %get-tuple-element.19.key_part_ref) | copy-start | bytes 9437188
  144.8 1.7 %copy-start.13 = (f32[768,1024]{1,0:T(8,128)}, f32[768,1024]{1,0:T(8,128)S(1)}, u32[]{:S(2)}) copy-start(f32[768,1024]{1,0:T(8,128)S(1)} %get-tuple-element.20.value_part_ref) | copy-start | bytes 9437188
  146.5 1.9 %copy-start.12 = (f32[768,1024]{1,0:T(8,128)S(1)}, f32[768,1024]{1,0:T(8,128)}, u32[]{:S(2)}) copy-start(f32[768,1024]{1,0:T(8,128)} %copy-done.11) | copy-start | bytes 9437188
  148.3 1.9 %copy-start.14 = (f32[768,1024]{1,0:T(8,128)S(1)}, f32[768,1024]{1,0:T(8,128)}, u32[]{:S(2)}) copy-start(f32[768,1024]{1,0:T(8,128)} %copy-done.13) | copy-start | bytes 9437188

commit v2 on v1

v2 whole, which is shorter than its diff:
```python
import functools

import jax
import jax.numpy as jnp
from jax import lax
from jax.experimental import pallas as pl
from jax.experimental.pallas import tpu as pltpu
from jax.sharding import PartitionSpec as P

HEAD_DIM = 128
UNIT = 256
SLICE = 16
VMEM = 58 * 1024 * 1024
SMALL_VMEM = 8 * 1024 * 1024
epsilon = 1e-06

F32 = jnp.float32
BF16 = jnp.bfloat16


def dot(left, right, contract):
    return lax.dot_general(
        left, right, ((contract[0:1], contract[1:2]), ((), ())), preferred_element_type=F32
    )


def unit(index):
    return slice(index * UNIT, (index + 1) * UNIT)


def columns(index):
    return slice(index * HEAD_DIM, (index + 1) * HEAD_DIM)


def causal():
    rows = lax.broadcasted_iota(jnp.int32, (UNIT, UNIT), 0)
    return rows >= lax.broadcasted_iota(jnp.int32, (UNIT, UNIT), 1)


def tile_mask(doc_ref, later, earlier):
    if later == earlier:
        return causal()
    return jnp.full((UNIT, UNIT), doc_ref[later * UNIT] == doc_ref[earlier * UNIT])


def masked_rows(keep, rows):
    return jnp.where(jnp.full(rows.shape, keep), rows, jnp.zeros_like(rows))


def column_of(row):
    return jnp.transpose(jnp.broadcast_to(row, (HEAD_DIM, row.shape[1])))


def tail_kernel(heads, doc_ref, place_ref, key_ref, value_ref, theirs_ref, mine_ref):
    tokens = key_ref.shape[0]
    last = doc_ref[tokens - 1]
    step = pl.program_id(0)
    half = pl.num_programs(0) // 2
    size = heads * HEAD_DIM // SLICE
    flag = jnp.where(last >= place_ref[0], 0.0, 1.0).astype(F32)
    states = []
    for h in range(heads):
        total = jnp.zeros((HEAD_DIM, HEAD_DIM), F32)
        for u in range(tokens // UNIT):
            key = masked_rows(doc_ref[u * UNIT] == last, key_ref[unit(u), columns(h)])
            total += dot(key, value_ref[unit(u), columns(h)], (0, 0))
        states.append(total)
    parts = jnp.concatenate(states, 0).reshape(size, SLICE, HEAD_DIM)

    @pl.when(step < half)
    def _():
        theirs_ref[pl.ds(step * size, size)] = parts
        theirs_ref[half * size] = jnp.full((SLICE, HEAD_DIM), flag)

    @pl.when(step >= half)
    def _():
        mine_ref[pl.ds((step - half) * size, size)] = parts
        mine_ref[half * size] = jnp.full((SLICE, HEAD_DIM), flag)


def combine_kernel(first_core, place_ref, mine_ref, theirs_ref, total_ref):
    rows = total_ref.shape[0]
    my_flag, their_flag = mine_ref[rows, 0:1, :], theirs_ref[rows, 0:1, :]
    first = jnp.full((SLICE, HEAD_DIM), place_ref[1] == first_core)
    for i in range(rows):
        mine, theirs = mine_ref[i], theirs_ref[i]
        total_ref[i, 0:SLICE, :] = jnp.where(
            first, theirs + their_flag * mine, mine + my_flag * theirs
        )
    if total_ref.shape[1] > SLICE:
        total_ref[:, SLICE:, :] = jnp.broadcast_to(my_flag * their_flag, (rows, 8, HEAD_DIM))


def spread_kernel(first_core, place_ref, entering_ref, mine_ref, theirs_ref, own_ref, other_ref):
    rows = entering_ref.shape[0]
    my_flag, their_flag = mine_ref[rows, 0:1, :], theirs_ref[rows, 0:1, :]
    first = jnp.full((SLICE, HEAD_DIM), place_ref[1] == first_core)
    for i in range(rows):
        entering = entering_ref[i]
        place = slice(i * SLICE, (i + 1) * SLICE)
        own_ref[place, :] = jnp.where(first, entering, theirs_ref[i] + their_flag * entering)
        other_ref[place, :] = jnp.where(first, mine_ref[i] + my_flag * entering, entering)


def scan_kernel(reverse, part_ref, flag_ref, state_ref):
    count = part_ref.shape[0]
    carry = jnp.zeros((SLICE, HEAD_DIM), F32)
    for step in range(count):
        b = count - 1 - step if reverse else step
        state_ref[b] = carry
        carry = part_ref[b, 0:SLICE, :] + flag_ref[b, SLICE : SLICE + 1, :] * carry


def pick(place_ref, mine_ref, theirs_ref, h):
    is_mine = pl.program_id(0) // (pl.num_programs(0) // 2) == place_ref[1]
    rows = slice(h * HEAD_DIM, (h + 1) * HEAD_DIM)
    keep = jnp.full((HEAD_DIM, HEAD_DIM), is_mine)
    return jnp.where(keep, mine_ref[rows, :], theirs_ref[rows, :]).astype(BF16)


def attended_kernel(heads, doc_ref, place_ref, query_ref, local_ref, cotangent_ref, gain_ref,
                    mine_ref, theirs_ref, out_ref, sums_ref, square, cross):
    tokens = query_ref.shape[0]
    offset = place_ref[0]
    step = pl.program_id(0)

    @pl.when(step == 0)
    def _():
        square[...] = jnp.zeros_like(square)
        cross[...] = jnp.zeros_like(cross)

    for u in range(tokens // UNIT):
        squares = square[unit(u), :]
        crosses = cross[unit(u), :]
        for h in range(heads):
            query = masked_rows(doc_ref[u * UNIT] < offset, query_ref[unit(u), columns(h)])
            prefix = pick(place_ref, mine_ref, theirs_ref, h)
            out = local_ref[unit(u), columns(h)] + dot(query, prefix, (1, 0))
            out_ref[unit(u), columns(h)] = out
            scaled = gain_ref[0:1, columns(h)] * cotangent_ref[unit(u), columns(h)].astype(F32)
            squares += out * out
            crosses += scaled * out
        square[unit(u), :] = squares
        cross[unit(u), :] = crosses

    @pl.when(step == pl.num_programs(0) - 1)
    def _():
        sums_ref[0:1, :] = jnp.sum(jnp.transpose(square[...]), axis=0, keepdims=True)
        sums_ref[1:2, :] = jnp.sum(jnp.transpose(cross[...]), axis=0, keepdims=True)


def norm_kernel(heads, features, doc_ref, place_ref, sums_ref, sums1_ref, sums2_ref, sums3_ref,
                out_ref, query_ref, cotangent_ref, gain_ref, normed_ref, grad_ref, theirs_ref, mine_ref, inverse, factor):
    tokens = query_ref.shape[0]
    step = pl.program_id(0)
    half = pl.num_programs(0) // 2
    size = heads * HEAD_DIM // SLICE
    flag = jnp.where(doc_ref[tokens - 1] >= place_ref[0], 0.0, 1.0).astype(F32)

    @pl.when(step == 0)
    def _():
        sums = sums_ref[...] + sums1_ref[...] + sums2_ref[...] + sums3_ref[...]
        inv = lax.rsqrt(sums[0:1] / features + epsilon)
        inverse[...] = column_of(inv)
        factor[...] = column_of(inv * inv * sums[1:2] / features)

    states = []
    for h in range(heads):
        total = jnp.zeros((HEAD_DIM, HEAD_DIM), F32)
        for u in range(tokens // UNIT):
            out = out_ref[unit(u), columns(h)]
            gain = gain_ref[0:1, columns(h)]
            inv = inverse[unit(u), :]
            normed_ref[unit(u), columns(h)] = (out * inv * gain).astype(BF16)
            scaled = gain * cotangent_ref[unit(u), columns(h)].astype(F32)
            grad = (inv * (scaled - out * factor[unit(u), :])).astype(BF16)
            grad_ref[unit(u), columns(h)] = grad
            query = masked_rows(doc_ref[u * UNIT] < place_ref[0], query_ref[unit(u), columns(h)])
            total += dot(query, grad, (0, 0))
        states.append(total)
    parts = jnp.concatenate(states, 0).reshape(size, SLICE, HEAD_DIM)

    @pl.when(step < half)
    def _():
        theirs_ref[pl.ds(step * size, size)] = parts
        theirs_ref[half * size] = jnp.full((SLICE, HEAD_DIM), flag)

    @pl.when(step >= half)
    def _():
        mine_ref[pl.ds((step - half) * size, size)] = parts
        mine_ref[half * size] = jnp.full((SLICE, HEAD_DIM), flag)


def rows_from(unit_index):
    return slice(unit_index * UNIT, None)


def lower_scores(doc_ref, left_ref, right_ref, s, h):
    scores = dot(left_ref[rows_from(s), columns(h)], right_ref[unit(s), columns(h)], (1, 1))
    units = left_ref.shape[0] // UNIT
    tiles = [
        jnp.where(tile_mask(doc_ref, t, s), scores[unit(t - s)], 0.0).astype(BF16)
        for t in range(s, units)
    ]
    return jnp.concatenate(tiles, 0)


def local_kernel(heads, doc_ref, query_ref, key_ref, value_ref, out_ref):
    for h in range(heads):
        for s in range(query_ref.shape[0] // UNIT):
            attend = lower_scores(doc_ref, query_ref, key_ref, s, h)
            part = dot(attend, value_ref[unit(s), columns(h)], (1, 0))
            if s == 0:
                out_ref[:, columns(h)] = part
            else:
                out_ref[rows_from(s), columns(h)] += part


def back_kernel(heads, doc_ref, place_ref, query_ref, key_ref, value_ref, grad_ref, mine_ref,
                theirs_ref, grad_q_ref, key_part_ref, grad_q):
    units = query_ref.shape[0] // UNIT
    for h in range(heads):
        prefix = pick(place_ref, mine_ref, theirs_ref, h)
        for t in range(units):
            carried = masked_rows(doc_ref[t * UNIT] < place_ref[0], grad_ref[unit(t), columns(h)])
            grad_q[unit(t), columns(h)] = dot(carried, prefix, (1, 1))
        for s in range(units):
            backs = lower_scores(doc_ref, grad_ref, value_ref, s, h)
            grad_q[rows_from(s), columns(h)] += dot(backs, key_ref[unit(s), columns(h)], (1, 0))
            key_part_ref[unit(s), columns(h)] = dot(
                backs, query_ref[rows_from(s), columns(h)], (0, 0)
            )
        grad_q_ref[:, columns(h)] = grad_q[:, columns(h)].astype(BF16)


def value_kernel(heads, doc_ref, query_ref, key_ref, grad_ref, value_part_ref):
    for h in range(heads):
        for s in range(query_ref.shape[0] // UNIT):
            attend = lower_scores(doc_ref, query_ref, key_ref, s, h)
            value_part_ref[unit(s), columns(h)] = dot(
                attend, grad_ref[rows_from(s), columns(h)], (0, 0)
            )


def finish_kernel(heads, doc_ref, place_ref, key_ref, value_ref, key_part_ref, value_part_ref,
                  mine_ref, theirs_ref, grad_k_ref, grad_v_ref):
    tokens = key_ref.shape[0]
    last = doc_ref[tokens - 1]
    for h in range(heads):
        suffix = pick(place_ref, mine_ref, theirs_ref, h)
        for u in range(tokens // UNIT):
            closing = doc_ref[u * UNIT] == last
            value = masked_rows(closing, value_ref[unit(u), columns(h)])
            grad_k = key_part_ref[unit(u), columns(h)] + dot(value, suffix, (1, 1))
            grad_k_ref[unit(u), columns(h)] = grad_k.astype(BF16)
            key = masked_rows(closing, key_ref[unit(u), columns(h)])
            grad_v = value_part_ref[unit(u), columns(h)] + dot(key, suffix, (1, 0))
            grad_v_ref[unit(u), columns(h)] = grad_v.astype(BF16)


def on_device(queries, keys, values, cotangent, norm_gain, doc_start):
    tokens, width = queries.shape
    blocks = lax.axis_size("seq")
    chips = blocks // 2
    heads = width // HEAD_DIM
    per_step = 2
    steps = heads // per_step
    features = width * lax.axis_size("head")
    gain = norm_gain.reshape(1, width)
    block = lax.axis_index("seq")
    core = block % 2
    place = jnp.stack([block * tokens, core]).astype(jnp.int32)

    def straight(i, place_ref):
        return i

    def theirs_first(i, place_ref):
        return per_step * ((i // 2) ^ (1 - place_ref[1])) + i % 2

    step_cols = per_step * HEAD_DIM
    docs = pl.BlockSpec(memory_space=pltpu.SMEM)

    def wide(order):
        return pl.BlockSpec((tokens, step_cols), lambda i, p: (0, order(i, p)))

    def gains(order):
        return pl.BlockSpec((1, step_cols), lambda i, p: (0, order(i, p)))

    def whole(*shape):
        return pl.BlockSpec(shape, lambda i, p: (0,) * len(shape))

    halves = pl.BlockSpec((step_cols, HEAD_DIM), lambda i, p: (i % 2, 0))
    tall = jax.ShapeDtypeStruct((tokens, width), F32)
    narrow = jax.ShapeDtypeStruct((tokens, width), BF16)

    def state(*shape):
        return jax.ShapeDtypeStruct(shape, F32)

    def call(kernel, ins, outs, shapes, products, arrays, scratch=()):
        def body(place_ref, doc_ref, *refs):
            kernel(doc_ref, place_ref, *refs)

        return functools.partial(
            pl.pallas_call(
                body,
                grid_spec=pltpu.PrefetchScalarGridSpec(
                    num_scalar_prefetch=1,
                    grid=(steps,),
                    in_specs=[docs] + ins,
                    out_specs=outs,
                    scratch_shapes=list(scratch),
                ),
                out_shape=shapes,
                cost_estimate=pl.CostEstimate(
                    flops=2 * products * tokens * width,
                    bytes_accessed=arrays * tokens * width,
                    transcendentals=0,
                ),
                compiler_params=pltpu.CompilerParams(vmem_limit_bytes=VMEM),
            ),
            place,
            doc_start,
        )

    def placeless(kernel):
        return lambda doc_ref, place_ref, *refs: kernel(doc_ref, *refs)

    rows = heads // 2 * HEAD_DIM // SLICE
    theirs, mine = call(
        functools.partial(tail_kernel, per_step),
        [wide(theirs_first), wide(theirs_first)],
        [whole(rows + 1, SLICE, HEAD_DIM)] * 2,
        [state(rows + 1, SLICE, HEAD_DIM)] * 2,
        HEAD_DIM,
        5,
    )(keys, values)

    def sibling(data):
        return lax.ppermute(data, "seq", [(i, i ^ 1) for i in range(blocks)])

    groups = [[2 * chip + c for chip in range(chips)] for c in range(2)]

    def exchange(data):
        return lax.all_to_all(data, "seq", 0, 0, axis_index_groups=groups)

    def small(kernel, shapes, *operands):
        return pl.pallas_call(
            kernel,
            in_specs=[
                pl.BlockSpec(memory_space=pltpu.SMEM if operand is place else pltpu.VMEM)
                for operand in operands
            ],
            out_shape=shapes,
            compiler_params=pltpu.CompilerParams(vmem_limit_bytes=SMALL_VMEM),
        )(*operands)

    def scan(part, flags, reverse):
        kernel = functools.partial(scan_kernel, reverse)
        return small(kernel, state(rows, SLICE, HEAD_DIM), part, flags)

    def combine(first_core, mine, received, depth):
        kernel = functools.partial(combine_kernel, first_core)
        return small(kernel, state(rows, depth, HEAD_DIM), place, mine, received)

    def spread(first_core, entering, mine, received):
        kernel = functools.partial(spread_kernel, first_core)
        shape = state(rows * SLICE, HEAD_DIM)
        own, other = small(kernel, [shape, shape], place, entering, mine, received)
        return own, sibling(other)

    received = sibling(theirs)
    flags = exchange(combine(0, mine, received, SLICE + 8))
    entering = exchange(scan(flags, flags, False))
    local = call(
        placeless(functools.partial(local_kernel, per_step)),
        [wide(straight)] * 3,
        wide(straight),
        tall,
        2 * 512,
        10,
    )(queries, keys, values)

    entering, local = lax.optimization_barrier((entering, local))
    prefix = spread(0, entering, mine, received)

    partial_rows = pltpu.VMEM((tokens, HEAD_DIM), F32)
    attended, sums = call(
        functools.partial(attended_kernel, per_step),
        [wide(straight)] * 3 + [gains(straight), halves, halves],
        [wide(straight), whole(2, tokens)],
        [tall, state(2, tokens)],
        HEAD_DIM,
        12,
        [partial_rows, partial_rows],
    )(queries, local, cotangent, gain, *prefix)

    count = lax.axis_size("head")
    all_sums = [sums] + [
        lax.ppermute(sums, "head", [(i, (i + step) % count) for i in range(count)])
        for step in range(1, count)
    ]
    normed, grad_out, theirs, mine = call(
        functools.partial(norm_kernel, per_step, features),
        [whole(2, tokens)] * count + [wide(theirs_first)] * 3 + [gains(theirs_first)],
        [wide(theirs_first)] * 2 + [whole(rows + 1, SLICE, HEAD_DIM)] * 2,
        [narrow, narrow] + [state(rows + 1, SLICE, HEAD_DIM)] * 2,
        HEAD_DIM,
        13,
        [partial_rows, partial_rows],
    )(*all_sums, attended, queries, cotangent, gain)

    received = sibling(theirs)
    gathered = exchange(combine(1, mine, received, SLICE))
    grad_q, key_part = call(
        functools.partial(back_kernel, per_step),
        [wide(straight)] * 4 + [halves, halves],
        [wide(straight)] * 2,
        [narrow, tall],
        3 * 512 + HEAD_DIM,
        14,
        [pltpu.VMEM((tokens, step_cols), F32)],
    )(queries, keys, values, grad_out, *prefix)
    gathered, grad_q, key_part = lax.optimization_barrier((gathered, grad_q, key_part))
    entering = exchange(scan(gathered, flags, True))
    value_part = call(
        placeless(functools.partial(value_kernel, per_step)),
        [wide(straight)] * 3,
        wide(straight),
        tall,
        2 * 512,
        10,
    )(queries, keys, grad_out)
    entering, value_part = lax.optimization_barrier((entering, value_part))
    suffix = spread(1, entering, mine, received)

    grad_k, grad_v = call(
        functools.partial(finish_kernel, per_step),
        [wide(straight)] * 4 + [halves, halves],
        [wide(straight)] * 2,
        [narrow, narrow],
        2 * HEAD_DIM,
        16,
    )(keys, values, key_part, value_part, *suffix)
    return normed, grad_q, grad_k, grad_v


def solution(mesh):
    wide = P("seq", "head")
    return jax.shard_map(
        on_device,
        mesh=mesh,
        in_specs=(wide, wide, wide, wide, P("head"), P("seq")),
        out_specs=(wide, wide, wide, wide),
        check_vma=False,
    )
```

time: 156 us -> 138 us (0.88)
  blocking collectives: 61.1 us -> 20.9 us
  starting transfers between devices: 16.7 us -> 38.9 us
  local copies, waits for them, and re-layouts: 23.9 us -> 5.36 us
  Pallas kernels: 42.6 us -> 59.6 us
    all_to_all x2 -> x1, blocking collectives: 61.1 us -> 20.9 us  [exchange(): return lax.all_to_all(data, 'seq', 0, 0, axis_index_groups=groups)]
    unnamed x42 -> x30, local copies, waits for them, and re-layouts: 23.2 us -> 5.36 us
    pallas_call x8 -> x13, Pallas kernels: 42.6 us -> 59.6 us  [the longest x1 12.2 us: on_device(): call(functools.partial(back_kernel, per_step), [wide(straight)] * 4 + [ha...]
    ppermute x0 -> x4, starting transfers between devices: none -> 12.6 us  [sibling(): return lax.ppermute(data, 'seq', [(i, i ^ 1) for i in range(blocks)])]
    all_to_all x2 -> x3, starting transfers between devices: 12.9 us -> 22.5 us  [exchange(): return lax.all_to_all(data, 'seq', 0, 0, axis_index_groups=groups)]
    ppermute x0 -> x4, waiting for transfers between devices: none -> 5.09 us  [sibling(): return lax.ppermute(data, 'seq', [(i, i ^ 1) for i in range(blocks)])]
    all_to_all x2 -> x3, waiting for transfers between devices: 6.88 us -> 2.33 us  [exchange(): return lax.all_to_all(data, 'seq', 0, 0, axis_index_groups=groups)]
  transfers between devices with their start and end apart: 5 -> 10, of which waited for: 3 -> 8; matrix products, arithmetic and copies ran while one was open for 0% -> 0% of each run, Pallas kernels for 15% -> 21%
where the time goes in v2:
time: 138 us; the launch traced here: 137 us
  Pallas kernels  59.6 us (43%)
  starting transfers between devices  38.9 us (28%)
  blocking collectives  20.9 us (15%)
  waiting for transfers between devices  10.6 us (8%)
  local copies, waits for them, and re-layouts  5.36 us (4%)
    all_to_all x3, starting transfers between devices, exchange(): return lax.all_to_all(data, 'seq', 0, 0, axis_index_groups=groups)  22.5 us
    all_to_all x1, blocking collectives, exchange(): return lax.all_to_all(data, 'seq', 0, 0, axis_index_groups=groups)  20.9 us
    ppermute x4, starting transfers between devices, sibling(): return lax.ppermute(data, 'seq', [(i, i ^ 1) for i in range(blocks)])  12.6 us
    pallas_call x1, Pallas kernels, on_device(): call(functools.partial(back_kernel, per_step), [wide(straight)] * 4 + [ha...  12.2 us
    pallas_call x1, Pallas kernels, on_device(): call(placeless(functools.partial(value_kernel, per_step)), [wide(straight...  8.82 us
    pallas_call x1, Pallas kernels, on_device(): call(placeless(functools.partial(local_kernel, per_step)), [wide(straight...  7.94 us
    pallas_call x1, Pallas kernels, on_device(): call(functools.partial(finish_kernel, per_step), [wide(straight)] * 4 + [...  7.16 us
    pallas_call x1, Pallas kernels, on_device(): call(functools.partial(norm_kernel, per_step, features), [whole(2, tokens...  7.08 us
  transfers between devices with their start and end apart: 10, of which 8 were waited for; matrix products, arithmetic and copies ran while one was open for 0% of the time, Pallas kernels for 21%

profile of v2, /device:TPU:1, one launch (start us, length us, event | category | flops | bytes accessed | tf_op | source)
XLA Modules:
  0.0 136.7 jit_solution(6283331211299981260)
XLA Ops:
  0.6 0.6 pad_add_fusion.place_ref
  1.3 0.0 copy-start.6
  1.3 5.0 %shard_map.93 = (f32[33,16,128]{2,1,0:T(8,128)}, f32[33,16,128]{2,1,0:T(8,128)}) custom-call(s32[2]{0:T(128)} %pad_add_fusion.place_ref, s32[768]{0:T(1024)} %doc_ref.13, bf16[768,1024]{1,0:T(8,128)(2,1)} %refs_0_.11, bf16[768,1024]{1,0:T(8,128)(2,1)} %refs_1_.9), custom_call_target="tpu_custom_call" | custom-call | flops 201326592 | bytes 3932160 | tf_op jit(solution)/shard_map/pallas_call | solution.py:329
  6.3 3.2 %collective-permute-start = (f32[33,16,128]{2,1,0:T(8,128)}, f32[33,16,128]{2,1,0:T(8,128)S(1)}, u32[]{:S(2)}, u32[]{:S(2)}) collective-permute-start(f32[33,16,128]{2,1,0:T(8,128)} %get-tuple-element.28), channel_id=1, source_target_pairs={{0,4},{4,0},{8,12},{12,8},{16,20},{20,16},{24,28},{28,24},{32,36},... | collective-permute-start | bytes 811016 | tf_op jit(solution)/shard_map/ppermute | solution.py:339
  9.5 1.4 %collective-permute-done.theirs_ref = f32[33,16,128]{2,1,0:T(8,128)S(1)} collective-permute-done((f32[33,16,128]{2,1,0:T(8,128)}, f32[33,16,128]{2,1,0:T(8,128)S(1)}, u32[]{:S(2)}, u32[]{:S(2)}) %collective-permute-start) | collective-permute-done | bytes 270368 | tf_op jit(solution)/shard_map/ppermute | solution.py:339
  10.9 0.0 copy-done.6
  10.9 0.0 copy-start
  10.9 1.0 copy-done
  11.8 0.6 shard_map.94
  12.4 20.9 %all_to_all.20.part_ref.flag_ref = f32[32,24,128]{2,1,0:T(8,128)S(1)} all-to-all(f32[32,24,128]{2,1,0:T(8,128)S(1)} %shard_map.94), channel_id=1, replica_groups={{0,8,16,24,32,40,48,56,64,72,80,88,96,104,112,120,128,136,144,152,160,1..., dimensions={0} | all-to-all | bytes 786432 | tf_op jit(solution)/shard_map/all_to_all | solution.py:344
  33.3 0.8 shard_map.95
  34.1 7.6 %all-to-all-start.1 = ((f32[32,16,128]{2,1,0:T(8,128)}), f32[32,16,128]{2,1,0:T(8,128)S(1)}, u32[]{:S(2)}, u32[]{:S(2)}) async-start(f32[32,16,128]{2,1,0:T(8,128)} %shard_map.95), calls=%async_computation.1 | async-start | bytes 524288 | tf_op jit(solution)/shard_map/all_to_all | solution.py:344
  41.7 0.0 copy-start.1
  41.7 0.0 copy-start.7
  41.7 7.9 %shard_map.96.refs_1_ = f32[768,1024]{1,0:T(8,128)} custom-call(s32[2]{0:T(128)} %pad_add_fusion.place_ref, s32[768]{0:T(1024)} %doc_ref.13, bf16[768,1024]{1,0:T(8,128)(2,1)} %refs_0_.10, bf16[768,1024]{1,0:T(8,128)(2,1)} %refs_0_.11, bf16[768,1024]{1,0:T(8,128)(2,1)} %refs_1_.9), custom_call_target="tpu_custom_call" | custom-call | flops 1610612736 | bytes 7864320 | tf_op jit(solution)/shard_map/pallas_call | solution.py:374
  49.6 1.7 %all-to-all-done.1.entering_ref = f32[32,16,128]{2,1,0:T(8,128)S(1)} async-done(((f32[32,16,128]{2,1,0:T(8,128)}), f32[32,16,128]{2,1,0:T(8,128)S(1)}, u32[]{:S(2)}, u32[]{:S(2)}) %all-to-all-start.1) | async-done | bytes 262176 | tf_op jit(solution)/shard_map/all_to_all | solution.py:344
  51.3 0.0 copy-done.1
  51.3 0.0 copy-done.7
  51.3 0.6 shard_map.97
  51.9 0.0 copy-start.4
  52.0 0.7 copy-done.4
  52.7 3.6 %collective-permute-start.1 = (f32[512,128]{1,0:T(8,128)S(1)}, f32[512,128]{1,0:T(8,128)S(1)}, u32[]{:S(2)}, u32[]{:S(2)}) collective-permute-start(f32[512,128]{1,0:T(8,128)S(1)} %get-tuple-element.32), channel_id=1, source_target_pairs={{0,4},{4,0},{8,12},{12,8},{16,20},{20,16},{24,28},{28,24},{32,36},... | collective-permute-start | bytes 786440 | tf_op jit(solution)/shard_map/ppermute | solution.py:339
  56.3 1.2 collective-permute-done.1.refs_5_
  57.4 0.0 copy-start.10
  57.5 0.7 copy-done.10
  58.1 6.7 %shard_map.98 = (f32[768,1024]{1,0:T(8,128)}, f32[2,768]{1,0:T(2,128)}) custom-call(s32[2]{0:T(128)} %pad_add_fusion.place_ref, s32[768]{0:T(1024)} %doc_ref.13, bf16[768,1024]{1,0:T(8,128)(2,1)} %refs_0_.10, f32[768,1024]{1,0:T(8,128)} %shard_map.96.refs_1_, bf16[768,1024]{1,0:T(8,128)(2,1)} %refs_6_.1, f32[1,1024]{1,0:T(1,128)} %bitcast.3, ...), custom_call_target="tpu_custom_call" | custom-call | flops 201326592 | bytes 9437184 | tf_op jit(solution)/shard_map/pallas_call | solution.py:387
  64.9 2.7 %collective-permute-start.4 = (f32[2,768]{1,0:T(2,128)}, f32[2,768]{1,0:T(2,128)S(1)}, u32[]{:S(2)}, u32[]{:S(2)}) collective-permute-start(f32[2,768]{1,0:T(2,128)} %get-tuple-element.33.refs_0_), channel_id=1, source_target_pairs={{0,3},{1,0},{2,1},{3,2},{4,7},{5,4},{6,5},{7,6},{8,11},{9,8},{10,9... | collective-permute-start | bytes 18440 | tf_op jit(solution)/shard_map/ppermute | solution.py:399
  67.6 0.3 collective-permute-start.3
  68.0 0.7 collective-permute-start.2
  68.7 0.0 collective-permute-done.4.refs_3_
  68.7 0.0 copy-start.12
  68.7 3.1 %collective-permute-done.3.refs_2_ = f32[2,768]{1,0:T(2,128)S(1)} collective-permute-done((f32[2,768]{1,0:T(2,128)}, f32[2,768]{1,0:T(2,128)S(1)}, u32[]{:S(2)}, u32[]{:S(2)}) %collective-permute-start.3) | collective-permute-done | bytes 6176 | tf_op jit(solution)/shard_map/ppermute | solution.py:399
  71.8 0.0 copy-start.13
  71.8 0.1 collective-permute-done.2.refs_1_
  71.9 0.0 copy-start.14
  71.9 0.0 copy-done.12
  71.9 0.5 copy-done.13
  72.4 0.1 copy-done.14
  72.5 0.0 copy-start.8
  72.5 7.1 %shard_map.99 = (bf16[768,1024]{1,0:T(8,128)(2,1)}, bf16[768,1024]{1,0:T(8,128)(2,1)}, f32[33,16,128]{2,1,0:T(8,128)}, f32[33,16,128]{2,1,0:T(8,128)}) custom-call(s32[2]{0:T(128)} %pad_add_fusion.place_ref, s32[768]{0:T(1024)} %doc_ref.13, f32[2,768]{1,0:T(2,128)} %get-tuple-element.33.refs_0_, f32[2,768]{1,0:T(2,128)} %copy-done.14, f32[2,768]{1,0:T(2,128)} %copy-done.13, ...), custom_call_target="tpu_custom_call" | custom-call | flops 201326592 | bytes 10223616 | tf_op jit(solution)/shard_map/pallas_call | solution.py:402
  79.6 2.2 %collective-permute-start.5 = (f32[33,16,128]{2,1,0:T(8,128)}, f32[33,16,128]{2,1,0:T(8,128)S(1)}, u32[]{:S(2)}, u32[]{:S(2)}) collective-permute-start(f32[33,16,128]{2,1,0:T(8,128)} %get-tuple-element.37), channel_id=1, source_target_pairs={{0,4},{4,0},{8,12},{12,8},{16,20},{20,16},{24,28},{28,24},{32,36},... | collective-permute-start | bytes 811016 | tf_op jit(solution)/shard_map/ppermute | solution.py:339
  81.7 1.4 %collective-permute-done.5.theirs_ref = f32[33,16,128]{2,1,0:T(8,128)S(1)} collective-permute-done((f32[33,16,128]{2,1,0:T(8,128)}, f32[33,16,128]{2,1,0:T(8,128)S(1)}, u32[]{:S(2)}, u32[]{:S(2)}) %collective-permute-start.5) | collective-permute-done | bytes 270368 | tf_op jit(solution)/shard_map/ppermute | solution.py:339
  83.1 0.0 copy-done.8
  83.1 0.0 copy-start.2
  83.1 1.0 copy-done.2
  84.1 1.3 shard_map.100
  85.4 5.5 %all-to-all-start.2 = ((f32[32,16,128]{2,1,0:T(8,128)}), f32[32,16,128]{2,1,0:T(8,128)S(1)}, u32[]{:S(2)}, u32[]{:S(2)}) async-start(f32[32,16,128]{2,1,0:T(8,128)} %shard_map.100), calls=%async_computation.2 | async-start | bytes 524288 | tf_op jit(solution)/shard_map/all_to_all | solution.py:344
  90.8 12.2 %shard_map.101 = (bf16[768,1024]{1,0:T(8,128)(2,1)}, f32[768,1024]{1,0:T(8,128)}) custom-call(s32[2]{0:T(128)} %pad_add_fusion.place_ref, s32[768]{0:T(1024)} %doc_ref.13, bf16[768,1024]{1,0:T(8,128)(2,1)} %refs_0_.10, bf16[768,1024]{1,0:T(8,128)(2,1)} %refs_0_.11, bf16[768,1024]{1,0:T(8,128)(2,1)} %refs_1_.9, ...), custom_call_target="tpu_custom_call" | custom-call | flops 2617245696 | bytes 11010048 | tf_op jit(solution)/shard_map/pallas_call | solution.py:414
  103.1 0.0 all-to-all-done.2.part_ref
  103.1 0.8 shard_map.102
  103.9 9.4 %all-to-all-start.3 = ((f32[32,16,128]{2,1,0:T(8,128)}), f32[32,16,128]{2,1,0:T(8,128)S(1)}, u32[]{:S(2)}, u32[]{:S(2)}) async-start(f32[32,16,128]{2,1,0:T(8,128)} %shard_map.102), calls=%async_computation.3 | async-start | bytes 524288 | tf_op jit(solution)/shard_map/all_to_all | solution.py:344
  113.3 0.0 copy-start.3
  113.3 0.0 copy-start.9
  113.3 8.8 %shard_map.103.refs_3_ = f32[768,1024]{1,0:T(8,128)} custom-call(s32[2]{0:T(128)} %pad_add_fusion.place_ref, s32[768]{0:T(1024)} %doc_ref.13, bf16[768,1024]{1,0:T(8,128)(2,1)} %refs_0_.10, bf16[768,1024]{1,0:T(8,128)(2,1)} %refs_0_.11, bf16[768,1024]{1,0:T(8,128)(2,1)} %get-tuple-element.38.refs_3_.refs_2_), custom_call_target="tpu_custom_call" | custom-call | flops 1610612736 | bytes 7864320 | tf_op jit(solution)/shard_map/pallas_call | solution.py:425
  122.1 0.6 all-to-all-done.3.entering_ref
  122.8 0.0 copy-done.3
  122.8 0.0 copy-done.9
  122.8 0.6 shard_map.104
  123.4 0.0 copy-start.5
  123.4 0.7 copy-done.5
  124.1 3.6 %collective-permute-start.6 = (f32[512,128]{1,0:T(8,128)S(1)}, f32[512,128]{1,0:T(8,128)S(1)}, u32[]{:S(2)}, u32[]{:S(2)}) collective-permute-start(f32[512,128]{1,0:T(8,128)S(1)} %get-tuple-element.47), channel_id=1, source_target_pairs={{0,4},{4,0},{8,12},{12,8},{16,20},{20,16},{24,28},{28,24},{32,36},... | collective-permute-start | bytes 786440 | tf_op jit(solution)/shard_map/ppermute | solution.py:339
  127.7 1.2 collective-permute-done.6.refs_5_
  128.9 0.7 copy-done.11
  129.6 7.2 %shard_map.105 = (bf16[768,1024]{1,0:T(8,128)(2,1)}, bf16[768,1024]{1,0:T(8,128)(2,1)}) custom-call(s32[2]{0:T(128)} %pad_add_fusion.place_ref, s32[768]{0:T(1024)} %doc_ref.13, bf16[768,1024]{1,0:T(8,128)(2,1)} %refs_0_.11, bf16[768,1024]{1,0:T(8,128)(2,1)} %refs_1_.9, f32[768,1024]{1,0:T(8,128)} %get-tuple-element.42.refs_2_, ...), custom_call_target="tpu_custom_call" | custom-call | flops 402653184 | bytes 12582912 | tf_op jit(solution)/shard_map/pallas_call | solution.py:436
  (1 shorter events, 0.0 us)
Async XLA Ops:
  1.3 9.6 %copy-start.6 = (s32[2]{0:T(128)S(1)}, s32[2]{0:T(128)}, u32[]{:S(2)}) copy-start(s32[2]{0:T(128)} %pad_add_fusion.place_ref) | copy-start | bytes 28
  6.3 4.6 %collective-permute-start = (f32[33,16,128]{2,1,0:T(8,128)}, f32[33,16,128]{2,1,0:T(8,128)S(1)}, u32[]{:S(2)}, u32[]{:S(2)}) collective-permute-start(f32[33,16,128]{2,1,0:T(8,128)} %get-tuple-element.28), channel_id=1, source_target_pairs={{0,4},{4,0},{8,12},{12,8},{16,20},{20,16},{24,28},{28,24},{32,36},... | collective-permute-start | bytes 811016 | tf_op jit(solution)/shard_map/ppermute | solution.py:339
  10.9 1.0 copy-start
  34.1 17.2 %all-to-all-start.1 = ((f32[32,16,128]{2,1,0:T(8,128)}), f32[32,16,128]{2,1,0:T(8,128)S(1)}, u32[]{:S(2)}, u32[]{:S(2)}) async-start(f32[32,16,128]{2,1,0:T(8,128)} %shard_map.95), calls=%async_computation.1 | async-start | bytes 524288 | tf_op jit(solution)/shard_map/all_to_all | solution.py:344
  41.7 9.7 %copy-start.1 = (f32[33,16,128]{2,1,0:T(8,128)S(1)}, f32[33,16,128]{2,1,0:T(8,128)}, u32[]{:S(2)}) copy-start(f32[33,16,128]{2,1,0:T(8,128)} %get-tuple-element.27.mine_ref) | copy-start | bytes 811012
  41.7 9.7 %copy-start.7 = (s32[2]{0:T(128)S(1)}, s32[2]{0:T(128)}, u32[]{:S(2)}) copy-start(s32[2]{0:T(128)} %pad_add_fusion.place_ref) | copy-start | bytes 28
  51.9 0.7 copy-start.4
  52.7 4.8 %collective-permute-start.1 = (f32[512,128]{1,0:T(8,128)S(1)}, f32[512,128]{1,0:T(8,128)S(1)}, u32[]{:S(2)}, u32[]{:S(2)}) collective-permute-start(f32[512,128]{1,0:T(8,128)S(1)} %get-tuple-element.32), channel_id=1, source_target_pairs={{0,4},{4,0},{8,12},{12,8},{16,20},{20,16},{24,28},{28,24},{32,36},... | collective-permute-start | bytes 786440 | tf_op jit(solution)/shard_map/ppermute | solution.py:339
  57.4 0.7 copy-start.10
  64.9 3.8 %collective-permute-start.4 = (f32[2,768]{1,0:T(2,128)}, f32[2,768]{1,0:T(2,128)S(1)}, u32[]{:S(2)}, u32[]{:S(2)}) collective-permute-start(f32[2,768]{1,0:T(2,128)} %get-tuple-element.33.refs_0_), channel_id=1, source_target_pairs={{0,3},{1,0},{2,1},{3,2},{4,7},{5,4},{6,5},{7,6},{8,11},{9,8},{10,9... | collective-permute-start | bytes 18440 | tf_op jit(solution)/shard_map/ppermute | solution.py:399
  67.6 4.2 %collective-permute-start.3 = (f32[2,768]{1,0:T(2,128)}, f32[2,768]{1,0:T(2,128)S(1)}, u32[]{:S(2)}, u32[]{:S(2)}) collective-permute-start(f32[2,768]{1,0:T(2,128)} %get-tuple-element.33.refs_0_), channel_id=1, source_target_pairs={{0,2},{1,3},{2,0},{3,1},{4,6},{5,7},{6,4},{7,5},{8,10},{9,11},{10,... | collective-permute-start | bytes 18440 | tf_op jit(solution)/shard_map/ppermute | solution.py:399
  68.0 3.9 %collective-permute-start.2 = (f32[2,768]{1,0:T(2,128)}, f32[2,768]{1,0:T(2,128)S(1)}, u32[]{:S(2)}, u32[]{:S(2)}) collective-permute-start(f32[2,768]{1,0:T(2,128)} %get-tuple-element.33.refs_0_), channel_id=1, source_target_pairs={{0,1},{1,2},{2,3},{3,0},{4,5},{5,6},{6,7},{7,4},{8,9},{9,10},{10,1... | collective-permute-start | bytes 18440 | tf_op jit(solution)/shard_map/ppermute | solution.py:399
  68.7 3.2 %copy-start.12 = (f32[2,768]{1,0:T(2,128)}, f32[2,768]{1,0:T(2,128)S(1)}, u32[]{:S(2)}) copy-start(f32[2,768]{1,0:T(2,128)S(1)} %collective-permute-done.4.refs_3_) | copy-start | bytes 18436
  71.8 0.6 copy-start.13
  71.9 0.6 copy-start.14
  72.5 10.6 %copy-start.8 = (s32[2]{0:T(128)S(1)}, s32[2]{0:T(128)}, u32[]{:S(2)}) copy-start(s32[2]{0:T(128)} %pad_add_fusion.place_ref) | copy-start | bytes 28
  79.6 3.5 %collective-permute-start.5 = (f32[33,16,128]{2,1,0:T(8,128)}, f32[33,16,128]{2,1,0:T(8,128)S(1)}, u32[]{:S(2)}, u32[]{:S(2)}) collective-permute-start(f32[33,16,128]{2,1,0:T(8,128)} %get-tuple-element.37), channel_id=1, source_target_pairs={{0,4},{4,0},{8,12},{12,8},{16,20},{20,16},{24,28},{28,24},{32,36},... | collective-permute-start | bytes 811016 | tf_op jit(solution)/shard_map/ppermute | solution.py:339
  83.1 1.0 copy-start.2
  85.4 17.7 %all-to-all-start.2 = ((f32[32,16,128]{2,1,0:T(8,128)}), f32[32,16,128]{2,1,0:T(8,128)S(1)}, u32[]{:S(2)}, u32[]{:S(2)}) async-start(f32[32,16,128]{2,1,0:T(8,128)} %shard_map.100), calls=%async_computation.2 | async-start | bytes 524288 | tf_op jit(solution)/shard_map/all_to_all | solution.py:344
  103.9 18.9 %all-to-all-start.3 = ((f32[32,16,128]{2,1,0:T(8,128)}), f32[32,16,128]{2,1,0:T(8,128)S(1)}, u32[]{:S(2)}, u32[]{:S(2)}) async-start(f32[32,16,128]{2,1,0:T(8,128)} %shard_map.102), calls=%async_computation.3 | async-start | bytes 524288 | tf_op jit(solution)/shard_map/all_to_all | solution.py:344
  113.3 9.5 %copy-start.3 = (f32[33,16,128]{2,1,0:T(8,128)S(1)}, f32[33,16,128]{2,1,0:T(8,128)}, u32[]{:S(2)}) copy-start(f32[33,16,128]{2,1,0:T(8,128)} %get-tuple-element.36.mine_ref) | copy-start | bytes 811012
  113.3 9.5 %copy-start.9 = (s32[2]{0:T(128)S(1)}, s32[2]{0:T(128)}, u32[]{:S(2)}) copy-start(s32[2]{0:T(128)} %pad_add_fusion.place_ref) | copy-start | bytes 28
  123.4 0.7 copy-start.5
  124.1 4.8 %collective-permute-start.6 = (f32[512,128]{1,0:T(8,128)S(1)}, f32[512,128]{1,0:T(8,128)S(1)}, u32[]{:S(2)}, u32[]{:S(2)}) collective-permute-start(f32[512,128]{1,0:T(8,128)S(1)} %get-tuple-element.47), channel_id=1, source_target_pairs={{0,4},{4,0},{8,12},{12,8},{16,20},{20,16},{24,28},{28,24},{32,36},... | collective-permute-start | bytes 786440 | tf_op jit(solution)/shard_map/ppermute | solution.py:339
  128.9 0.7 copy-start.11

commit v3 on v2

v3 whole, which is shorter than its diff:
```python
import functools

import jax
import jax.numpy as jnp
from jax import lax
from jax.experimental import pallas as pl
from jax.experimental.pallas import tpu as pltpu
from jax.sharding import PartitionSpec as P

HEAD_DIM = 128
UNIT = 256
SLICE = 16
ROWS = 256
VMEM = 58 * 1024 * 1024
ROW_VMEM = 58 * 1024 * 1024
SMALL_VMEM = 8 * 1024 * 1024
epsilon = 1e-06

F32 = jnp.float32
BF16 = jnp.bfloat16


def dot(left, right, contract):
    return lax.dot_general(
        left, right, ((contract[0:1], contract[1:2]), ((), ())), preferred_element_type=F32
    )


def unit(index):
    return slice(index * UNIT, (index + 1) * UNIT)


def columns(index):
    return slice(index * HEAD_DIM, (index + 1) * HEAD_DIM)


def causal(later_dim=0):
    later = lax.broadcasted_iota(jnp.int32, (UNIT, UNIT), later_dim)
    return later >= lax.broadcasted_iota(jnp.int32, (UNIT, UNIT), 1 - later_dim)


def tile_mask(doc_ref, later, earlier):
    if later == earlier:
        return causal()
    return jnp.full((UNIT, UNIT), doc_ref[later * UNIT] == doc_ref[earlier * UNIT])


def masked_rows(keep, rows):
    return jnp.where(jnp.full(rows.shape, keep), rows, jnp.zeros_like(rows))


def column_of(row):
    return jnp.transpose(jnp.broadcast_to(row, (HEAD_DIM, row.shape[1])))


def add_state(total, left_ref, right_ref, keep, heads):
    for h in range(heads):
        left = masked_rows(keep, left_ref[:, columns(h)])
        total[columns(h), :] += dot(left, right_ref[:, columns(h)], (0, 0))


def split_state(total, doc_ref, place_ref, theirs_ref, mine_ref):
    rows = total.shape[0] // (2 * SLICE)
    flag = jnp.where(doc_ref[doc_ref.shape[0] - 1] >= place_ref[0], 0.0, 1.0).astype(F32)
    low = total[: rows * SLICE, :].reshape(rows, SLICE, HEAD_DIM)
    high = total[rows * SLICE :, :].reshape(rows, SLICE, HEAD_DIM)
    is_low = jnp.full(low.shape, place_ref[1] == 0)
    mine_ref[0:rows] = jnp.where(is_low, low, high)
    theirs_ref[0:rows] = jnp.where(is_low, high, low)
    mine_ref[rows] = jnp.full((SLICE, HEAD_DIM), flag)
    theirs_ref[rows] = jnp.full((SLICE, HEAD_DIM), flag)


def streamed(kernel, before, after, ins, outs):
    def body(doc_ref, place_ref, *refs):
        sources, rest = refs[:ins], refs[ins:]
        targets, rest = rest[-outs:] if outs else (), rest[: len(rest) - outs] if outs else rest
        buffers, sems = rest[-1 - ins - outs : -1], rest[-1]
        rest = rest[: -1 - ins - outs]
        bands = doc_ref.shape[0] // ROWS

        def copy(k, i):
            rows = pl.ds(i * ROWS, ROWS)
            if k < ins:
                ends = sources[k].at[rows], buffers[k].at[rows]
            else:
                ends = buffers[k].at[rows], targets[k - ins].at[rows]
            return pltpu.make_async_copy(*ends, sems.at[k, i])

        for i in range(bands):
            for k in range(ins):
                copy(k, i).start()
        if before is not None:
            before(doc_ref, place_ref, *rest)
        for i in range(bands):
            for k in range(ins):
                copy(k, i).wait()
            views = [b.at[pl.ds(i * ROWS, ROWS)] for b in buffers]
            kernel(i, doc_ref, place_ref, *views, *rest)
            for k in range(ins, ins + outs):
                copy(k, i).start()
        if after is not None:
            after(doc_ref, place_ref, *rest)
        for i in range(bands):
            for k in range(ins, ins + outs):
                copy(k, i).wait()

    return body


def add_state(total, left_ref, right_ref, keep, heads):
    for h in range(heads):
        left = masked_rows(keep, left_ref[:, columns(h)])
        total[columns(h), :] += dot(left, right_ref[:, columns(h)], (0, 0))


def split_state(doc_ref, place_ref, *refs):
    theirs_ref, mine_ref, total = refs[-3:]
    rows = total.shape[0] // (2 * SLICE)
    flag = jnp.where(doc_ref[doc_ref.shape[0] - 1] >= place_ref[0], 0.0, 1.0).astype(F32)
    low = total[: rows * SLICE, :].reshape(rows, SLICE, HEAD_DIM)
    high = total[rows * SLICE :, :].reshape(rows, SLICE, HEAD_DIM)
    is_low = jnp.full(low.shape, place_ref[1] == 0)
    mine_ref[0:rows] = jnp.where(is_low, low, high)
    theirs_ref[0:rows] = jnp.where(is_low, high, low)
    mine_ref[rows] = jnp.full((SLICE, HEAD_DIM), flag)
    theirs_ref[rows] = jnp.full((SLICE, HEAD_DIM), flag)


def clear_state(doc_ref, place_ref, *refs):
    refs[-1][...] = jnp.zeros_like(refs[-1])


def tail_kernel(heads, i, doc_ref, place_ref, key_ref, value_ref, theirs_ref, mine_ref, total):
    keep = doc_ref[i * ROWS] == doc_ref[doc_ref.shape[0] - 1]
    add_state(total, key_ref, value_ref, keep, heads)


def combine_kernel(first_core, place_ref, mine_ref, theirs_ref, total_ref):
    rows = total_ref.shape[0]
    my_flag, their_flag = mine_ref[rows, 0:1, :], theirs_ref[rows, 0:1, :]
    first = jnp.full((SLICE, HEAD_DIM), place_ref[1] == first_core)
    for i in range(rows):
        mine, theirs = mine_ref[i], theirs_ref[i]
        total_ref[i, 0:SLICE, :] = jnp.where(
            first, theirs + their_flag * mine, mine + my_flag * theirs
        )
    if total_ref.shape[1] > SLICE:
        total_ref[:, SLICE:, :] = jnp.broadcast_to(my_flag * their_flag, (rows, 8, HEAD_DIM))


def spread_kernel(first_core, place_ref, entering_ref, mine_ref, theirs_ref, own_ref, other_ref):
    rows = entering_ref.shape[0]
    my_flag, their_flag = mine_ref[rows, 0:1, :], theirs_ref[rows, 0:1, :]
    first = jnp.full((SLICE, HEAD_DIM), place_ref[1] == first_core)
    for i in range(rows):
        entering = entering_ref[i]
        place = slice(i * SLICE, (i + 1) * SLICE)
        own_ref[place, :] = jnp.where(first, entering, theirs_ref[i] + their_flag * entering)
        other_ref[place, :] = jnp.where(first, mine_ref[i] + my_flag * entering, entering)


def scan_kernel(reverse, part_ref, flag_ref, state_ref):
    count = part_ref.shape[0]
    carry = jnp.zeros((SLICE, HEAD_DIM), F32)
    for step in range(count):
        b = count - 1 - step if reverse else step
        state_ref[b] = carry
        carry = part_ref[b, 0:SLICE, :] + flag_ref[b, SLICE : SLICE + 1, :] * carry


def picked(place_ref, mine_ref, theirs_ref, is_mine, h):
    rows = slice(h * HEAD_DIM, (h + 1) * HEAD_DIM)
    keep = jnp.full((HEAD_DIM, HEAD_DIM), is_mine)
    return jnp.where(keep, mine_ref[rows, :], theirs_ref[rows, :]).astype(BF16)


def pick(place_ref, mine_ref, theirs_ref, h):
    is_mine = pl.program_id(0) // (pl.num_programs(0) // 2) == place_ref[1]
    return picked(place_ref, mine_ref, theirs_ref, is_mine, h)


def pick_head(place_ref, mine_ref, theirs_ref, heads, h):
    half = heads // 2
    return picked(place_ref, mine_ref, theirs_ref, place_ref[1] == h // half, h % half)


def attended_kernel(heads, i, doc_ref, place_ref, query_ref, local_ref, cotangent_ref, out_ref,
                    gain_ref, mine_ref, theirs_ref, sums_ref):
    carried = doc_ref[i * ROWS] < place_ref[0]
    squares = jnp.zeros((ROWS, HEAD_DIM), F32)
    crosses = jnp.zeros((ROWS, HEAD_DIM), F32)
    for h in range(heads):
        query = masked_rows(carried, query_ref[:, columns(h)])
        prefix = pick_head(place_ref, mine_ref, theirs_ref, heads, h)
        out = local_ref[:, columns(h)] + dot(query, prefix, (1, 0))
        out_ref[:, columns(h)] = out
        scaled = gain_ref[0:1, columns(h)] * cotangent_ref[:, columns(h)].astype(F32)
        squares += out * out
        crosses += scaled * out
    band = slice(i * ROWS, (i + 1) * ROWS)
    sums_ref[0:1, band] = jnp.sum(jnp.transpose(squares), axis=0, keepdims=True)
    sums_ref[1:2, band] = jnp.sum(jnp.transpose(crosses), axis=0, keepdims=True)


def norm_kernel(heads, features, i, doc_ref, place_ref, out_ref, query_ref, cotangent_ref,
                normed_ref, grad_ref, gain_ref, sums_ref, sums1_ref, sums2_ref, sums3_ref,
                theirs_ref, mine_ref, total):
    band = slice(i * ROWS, (i + 1) * ROWS)
    sums = sums_ref[:, band] + sums1_ref[:, band] + sums2_ref[:, band] + sums3_ref[:, band]
    inv_row = lax.rsqrt(sums[0:1] / features + epsilon)
    inv = column_of(inv_row)
    factor = column_of(inv_row * inv_row * sums[1:2] / features)
    for h in range(heads):
        out = out_ref[:, columns(h)]
        gain = gain_ref[0:1, columns(h)]
        normed_ref[:, columns(h)] = (out * inv * gain).astype(BF16)
        scaled = gain * cotangent_ref[:, columns(h)].astype(F32)
        grad_ref[:, columns(h)] = (inv * (scaled - out * factor)).astype(BF16)
    add_state(total, query_ref, grad_ref, doc_ref[i * ROWS] < place_ref[0], heads)


def rows_from(unit_index):
    return slice(unit_index * UNIT, None)


def lower_scores(doc_ref, left_ref, right_ref, s, h):
    scores = dot(left_ref[rows_from(s), columns(h)], right_ref[unit(s), columns(h)], (1, 1))
    units = left_ref.shape[0] // UNIT
    tiles = [
        jnp.where(tile_mask(doc_ref, t, s), scores[unit(t - s)], 0.0).astype(BF16)
        for t in range(s, units)
    ]
    return jnp.concatenate(tiles, 0)


def upper_scores(doc_ref, left_ref, right_ref, s, h):
    scores = dot(left_ref[unit(s), columns(h)], right_ref[rows_from(s), columns(h)], (1, 1))
    tiles = []
    for t in range(s, right_ref.shape[0] // UNIT):
        mask = tile_mask(doc_ref, t, s) if t > s else causal(1)
        tiles.append(jnp.where(mask, scores[:, unit(t - s)], 0.0).astype(BF16))
    return jnp.concatenate(tiles, 1)


def local_kernel(heads, doc_ref, query_ref, key_ref, value_ref, out_ref):
    for h in range(heads):
        for s in range(query_ref.shape[0] // UNIT):
            attend = lower_scores(doc_ref, query_ref, key_ref, s, h)
            part = dot(attend, value_ref[unit(s), columns(h)], (1, 0))
            if s == 0:
                out_ref[:, columns(h)] = part
            else:
                out_ref[rows_from(s), columns(h)] += part


def back_kernel(heads, doc_ref, place_ref, query_ref, key_ref, value_ref, grad_ref, mine_ref,
                theirs_ref, grad_q_ref, key_part_ref, grad_q):
    units = query_ref.shape[0] // UNIT
    for h in range(heads):
        prefix = pick(place_ref, mine_ref, theirs_ref, h)
        for t in range(units):
            carried = masked_rows(doc_ref[t * UNIT] < place_ref[0], grad_ref[unit(t), columns(h)])
            grad_q[unit(t), columns(h)] = dot(carried, prefix, (1, 1))
        for s in range(units):
            backs = lower_scores(doc_ref, grad_ref, value_ref, s, h)
            grad_q[rows_from(s), columns(h)] += dot(backs, key_ref[unit(s), columns(h)], (1, 0))
            key_part_ref[unit(s), columns(h)] = dot(
                backs, query_ref[rows_from(s), columns(h)], (0, 0)
            )
        grad_q_ref[:, columns(h)] = grad_q[:, columns(h)].astype(BF16)


def value_kernel(heads, doc_ref, query_ref, key_ref, grad_ref, value_part_ref):
    for h in range(heads):
        for s in range(query_ref.shape[0] // UNIT):
            attend = upper_scores(doc_ref, key_ref, query_ref, s, h)
            value_part_ref[unit(s), columns(h)] = dot(
                attend, grad_ref[rows_from(s), columns(h)], (1, 0)
            )


def finish_kernel(heads, i, doc_ref, place_ref, key_ref, value_ref, key_part_ref,
                  value_part_ref, grad_k_ref, grad_v_ref, mine_ref, theirs_ref):
    closing = doc_ref[i * ROWS] == doc_ref[doc_ref.shape[0] - 1]
    for h in range(heads):
        suffix = pick_head(place_ref, mine_ref, theirs_ref, heads, h)
        value = masked_rows(closing, value_ref[:, columns(h)])
        grad_k = key_part_ref[:, columns(h)] + dot(value, suffix, (1, 1))
        grad_k_ref[:, columns(h)] = grad_k.astype(BF16)
        key = masked_rows(closing, key_ref[:, columns(h)])
        grad_v = value_part_ref[:, columns(h)] + dot(key, suffix, (1, 0))
        grad_v_ref[:, columns(h)] = grad_v.astype(BF16)


def on_device(queries, keys, values, cotangent, norm_gain, doc_start):
    tokens, width = queries.shape
    blocks = lax.axis_size("seq")
    chips = blocks // 2
    heads = width // HEAD_DIM
    per_step = 2
    steps = heads // per_step
    features = width * lax.axis_size("head")
    gain = norm_gain.reshape(1, width)

    def here():
        block = lax.axis_index("seq")
        return block * tokens, lax.rem(block, 2)

    step_cols = per_step * HEAD_DIM
    docs = pl.BlockSpec(memory_space=pltpu.SMEM)

    wide = pl.BlockSpec((tokens, step_cols), lambda i: (0, i))
    anywhere = pl.BlockSpec(memory_space=pl.ANY)
    vmem = pl.BlockSpec(memory_space=pltpu.VMEM)

    def stream(kernel, arrays, operands, wide_outs, outs, products, traffic, before=None,
               after=None, scratch=()):
        ins, count = len(arrays), len(wide_outs)
        inner = streamed(kernel, before, after, ins, count)

        def body(doc_ref, *refs):
            front, rest = refs[: ins + len(operands)], refs[ins + len(operands) :]
            big, small_outs = rest[:count], rest[count : count + len(outs)]
            extra = rest[count + len(outs) :]
            own, buffers = extra[: len(scratch)], extra[len(scratch) :]
            inner(doc_ref, here(), *front, *small_outs, *own, *buffers, *big)

        return pl.pallas_call(
            body,
            in_specs=[docs] + [anywhere] * ins + [vmem] * len(operands),
            out_specs=[anywhere] * count + [vmem] * len(outs),
            out_shape=list(wide_outs) + list(outs),
            scratch_shapes=list(scratch)
            + [pltpu.VMEM(a.shape, a.dtype) for a in list(arrays) + list(wide_outs)]
            + [pltpu.SemaphoreType.DMA((ins + count, tokens // ROWS))],
            cost_estimate=pl.CostEstimate(
                flops=2 * products * tokens * width,
                bytes_accessed=traffic * tokens * width,
                transcendentals=0,
            ),
            compiler_params=pltpu.CompilerParams(vmem_limit_bytes=ROW_VMEM),
        )(doc_start, *arrays, *operands)

    halves = pl.BlockSpec((step_cols, HEAD_DIM), lambda i: (i % 2, 0))
    tall = jax.ShapeDtypeStruct((tokens, width), F32)
    narrow = jax.ShapeDtypeStruct((tokens, width), BF16)

    def state(*shape):
        return jax.ShapeDtypeStruct(shape, F32)

    def call(kernel, ins, outs, shapes, products, arrays, scratch=()):
        def body(doc_ref, *refs):
            kernel(doc_ref, here(), *refs)

        return functools.partial(
            pl.pallas_call(
                body,
                grid=(steps,),
                in_specs=[docs] + ins,
                out_specs=outs,
                scratch_shapes=list(scratch),
                out_shape=shapes,
                cost_estimate=pl.CostEstimate(
                    flops=2 * products * tokens * width,
                    bytes_accessed=arrays * tokens * width,
                    transcendentals=0,
                ),
                compiler_params=pltpu.CompilerParams(vmem_limit_bytes=VMEM),
            ),
            doc_start,
        )

    def placeless(kernel):
        return lambda doc_ref, place_ref, *refs: kernel(doc_ref, *refs)

    rows = heads // 2 * HEAD_DIM // SLICE
    total_rows = pltpu.VMEM((width, HEAD_DIM), F32)
    parted = [state(rows + 1, SLICE, HEAD_DIM)] * 2
    theirs, mine = stream(
        functools.partial(tail_kernel, heads),
        [keys, values], [], [], parted, HEAD_DIM, 5, clear_state, split_state, [total_rows],
    )

    def sibling(data):
        return lax.ppermute(data, "seq", [(i, i ^ 1) for i in range(blocks)])

    groups = [[2 * chip + c for chip in range(chips)] for c in range(2)]

    def exchange(data):
        return lax.all_to_all(data, "seq", 0, 0, axis_index_groups=groups)

    def small(kernel, shapes, *operands):
        return pl.pallas_call(
            kernel,
            out_shape=shapes,
            compiler_params=pltpu.CompilerParams(vmem_limit_bytes=SMALL_VMEM),
        )(*operands)

    def placed(kernel, first_core):
        return lambda *refs: kernel(first_core, here(), *refs)

    def scan(part, flags, reverse):
        kernel = functools.partial(scan_kernel, reverse)
        return small(kernel, state(rows, SLICE, HEAD_DIM), part, flags)

    def combine(first_core, mine, received, depth):
        kernel = placed(combine_kernel, first_core)
        return small(kernel, state(rows, depth, HEAD_DIM), mine, received)

    def spread(first_core, entering, mine, received):
        kernel = placed(spread_kernel, first_core)
        shape = state(rows * SLICE, HEAD_DIM)
        own, other = small(kernel, [shape, shape], entering, mine, received)
        return own, sibling(other)

    received = sibling(theirs)
    flags = exchange(combine(0, mine, received, SLICE + 8))
    entering = exchange(scan(flags, flags, False))
    local = call(
        placeless(functools.partial(local_kernel, per_step)),
        [wide] * 3,
        wide,
        tall,
        2 * 512,
        10,
    )(queries, keys, values)

    entering, local = lax.optimization_barrier((entering, local))
    prefix = spread(0, entering, mine, received)

    attended, sums = stream(
        functools.partial(attended_kernel, heads),
        [queries, local, cotangent], [gain, *prefix], [tall], [state(2, tokens)], HEAD_DIM, 12,
    )

    count = lax.axis_size("head")
    all_sums = [sums] + [
        lax.ppermute(sums, "head", [(i, (i + step) % count) for i in range(count)])
        for step in range(1, count)
    ]
    normed, grad_out, theirs, mine = stream(
        functools.partial(norm_kernel, heads, features),
        [attended, queries, cotangent], [gain, *all_sums], [narrow, narrow], parted, HEAD_DIM, 13,
        clear_state, split_state, [total_rows],
    )

    received = sibling(theirs)
    gathered = exchange(combine(1, mine, received, SLICE))
    grad_q, key_part = call(
        functools.partial(back_kernel, per_step),
        [wide] * 4 + [halves, halves],
        [wide] * 2,
        [narrow, tall],
        3 * 512 + HEAD_DIM,
        14,
        [pltpu.VMEM((tokens, step_cols), F32)],
    )(queries, keys, values, grad_out, *prefix)
    gathered, grad_q, key_part = lax.optimization_barrier((gathered, grad_q, key_part))
    entering = exchange(scan(gathered, flags, True))
    value_part = call(
        placeless(functools.partial(value_kernel, per_step)),
        [wide] * 3,
        wide,
        tall,
        2 * 512,
        10,
    )(queries, keys, grad_out)
    entering, value_part = lax.optimization_barrier((entering, value_part))
    suffix = spread(1, entering, mine, received)

    grad_k, grad_v = stream(
        functools.partial(finish_kernel, heads),
        [keys, values, key_part, value_part], [*suffix], [narrow, narrow], [], 2 * HEAD_DIM, 16,
    )
    return normed, grad_q, grad_k, grad_v


def solution(mesh):
    wide = P("seq", "head")
    return jax.shard_map(
        on_device,
        mesh=mesh,
        in_specs=(wide, wide, wide, wide, P("head"), P("seq")),
        out_specs=(wide, wide, wide, wide),
        check_vma=False,
    )
```

time: 138 us -> 130 us (0.942)
  Pallas kernels: 59.6 us -> 51.8 us
  waiting for transfers between devices: 10.6 us -> 12.6 us
    pallas_call x13, Pallas kernels: 59.6 us -> 51.8 us  [the longest x4 22.6 us: stream(): pl.pallas_call(body, in_specs=[docs] + [anywhere] * ins + [vmem] * len(op...]
    all_to_all x3, waiting for transfers between devices: 2.33 us -> 4.25 us  [exchange(): return lax.all_to_all(data, 'seq', 0, 0, axis_index_groups=groups)]
    unnamed x30 -> x22, local copies, waits for them, and re-layouts: 5.36 us -> 5.34 us
where the time goes in v3:
time: 130 us
  Pallas kernels  51.8 us (40%)
  starting transfers between devices  38 us (29%)
  blocking collectives  20.9 us (16%)
  waiting for transfers between devices  12.6 us (10%)
  local copies, waits for them, and re-layouts  5.34 us (4%)
    pallas_call x4, Pallas kernels, stream(): pl.pallas_call(body, in_specs=[docs] + [anywhere] * ins + [vmem] * len(op...  22.6 us
    all_to_all x3, starting transfers between devices, exchange(): return lax.all_to_all(data, 'seq', 0, 0, axis_index_groups=groups)  21.5 us
    all_to_all x1, blocking collectives, exchange(): return lax.all_to_all(data, 'seq', 0, 0, axis_index_groups=groups)  20.9 us
    ppermute x4, starting transfers between devices, sibling(): return lax.ppermute(data, 'seq', [(i, i ^ 1) for i in range(blocks)])  12.7 us
    pallas_call x1, Pallas kernels, on_device(): call(functools.partial(back_kernel, per_step), [wide] * 4 + [halves, halv...  11.6 us
    pallas_call x1, Pallas kernels, on_device(): call(placeless(functools.partial(value_kernel, per_step)), [wide] * 3, wi...  7.85 us
    pallas_call x1, Pallas kernels, on_device(): call(placeless(functools.partial(local_kernel, per_step)), [wide] * 3, wi...  7.19 us
    unnamed x22, local copies, waits for them, and re-layouts  5.34 us
  transfers between devices with their start and end apart: 10, of which 8 were waited for; matrix products, arithmetic and copies ran while one was open for 0% of the time, Pallas kernels for 21%

profile of v3, /device:TPU:1, one launch (start us, length us, event | category | flops | bytes accessed | tf_op | source)
XLA Modules:
  0.0 129.5 jit_solution(13861702006449728536)
XLA Ops:
  0.6 3.8 %shard_map.93 = (f32[33,16,128]{2,1,0:T(8,128)}, f32[33,16,128]{2,1,0:T(8,128)}) custom-call(s32[768]{0:T(1024)} %doc_ref.13, bf16[768,1024]{1,0:T(8,128)(2,1)} %refs_0_.11, bf16[768,1024]{1,0:T(8,128)(2,1)} %refs_1_.11), custom_call_target="tpu_custom_call" | custom-call | flops 201326592 | bytes 3932160 | tf_op jit(solution)/shard_map/pallas_call | solution.py:329
  4.5 3.3 %collective-permute-start = (f32[33,16,128]{2,1,0:T(8,128)}, f32[33,16,128]{2,1,0:T(8,128)S(1)}, u32[]{:S(2)}, u32[]{:S(2)}) collective-permute-start(f32[33,16,128]{2,1,0:T(8,128)} %get-tuple-element.28), channel_id=1, source_target_pairs={{0,4},{4,0},{8,12},{12,8},{16,20},{20,16},{24,28},{28,24},{32,36},... | collective-permute-start | bytes 811016 | tf_op jit(solution)/shard_map/ppermute | solution.py:386
  7.8 1.4 %collective-permute-done.refs_1_.refs_2_ = f32[33,16,128]{2,1,0:T(8,128)S(1)} collective-permute-done((f32[33,16,128]{2,1,0:T(8,128)}, f32[33,16,128]{2,1,0:T(8,128)S(1)}, u32[]{:S(2)}, u32[]{:S(2)}) %collective-permute-start) | collective-permute-done | bytes 270368 | tf_op jit(solution)/shard_map/ppermute | solution.py:386
  9.2 0.0 copy-start
  9.2 1.0 copy-done
  10.1 0.1 shard_map.94
  10.2 20.9 %all_to_all.20.part_ref.flag_ref = f32[32,24,128]{2,1,0:T(8,128)S(1)} all-to-all(f32[32,24,128]{2,1,0:T(8,128)S(1)} %shard_map.94), channel_id=1, replica_groups={{0,8,16,24,32,40,48,56,64,72,80,88,96,104,112,120,128,136,144,152,160,1..., dimensions={0} | all-to-all | bytes 786432 | tf_op jit(solution)/shard_map/all_to_all | solution.py:391
  31.1 0.8 shard_map.95
  31.9 7.6 %all-to-all-start.1 = ((f32[32,16,128]{2,1,0:T(8,128)}), f32[32,16,128]{2,1,0:T(8,128)S(1)}, u32[]{:S(2)}, u32[]{:S(2)}) async-start(f32[32,16,128]{2,1,0:T(8,128)} %shard_map.95), calls=%async_computation.1 | async-start | bytes 524288 | tf_op jit(solution)/shard_map/all_to_all | solution.py:391
  39.4 0.0 copy-start.1
  39.4 7.2 %shard_map.96.refs_1_ = f32[768,1024]{1,0:T(8,128)} custom-call(s32[768]{0:T(1024)} %doc_ref.13, bf16[768,1024]{1,0:T(8,128)(2,1)} %refs_0_.10, bf16[768,1024]{1,0:T(8,128)(2,1)} %refs_0_.11, bf16[768,1024]{1,0:T(8,128)(2,1)} %refs_1_.11), custom_call_target="tpu_custom_call" | custom-call | flops 1610612736 | bytes 7864320 | tf_op jit(solution)/shard_map/pallas_call | solution.py:420
  46.6 2.5 %all-to-all-done.1.refs_0_ = f32[32,16,128]{2,1,0:T(8,128)S(1)} async-done(((f32[32,16,128]{2,1,0:T(8,128)}), f32[32,16,128]{2,1,0:T(8,128)S(1)}, u32[]{:S(2)}, u32[]{:S(2)}) %all-to-all-start.1) | async-done | bytes 262176 | tf_op jit(solution)/shard_map/all_to_all | solution.py:391
  49.1 0.0 copy-done.1
  49.1 0.1 shard_map.97
  49.2 0.0 copy-start.5
  49.2 0.7 copy-done.5
  49.9 3.6 %collective-permute-start.1 = (f32[512,128]{1,0:T(8,128)S(1)}, f32[512,128]{1,0:T(8,128)S(1)}, u32[]{:S(2)}, u32[]{:S(2)}) collective-permute-start(f32[512,128]{1,0:T(8,128)S(1)} %get-tuple-element.32), channel_id=1, source_target_pairs={{0,4},{4,0},{8,12},{12,8},{16,20},{20,16},{24,28},{28,24},{32,36},... | collective-permute-start | bytes 786440 | tf_op jit(solution)/shard_map/ppermute | solution.py:386
  53.5 1.2 collective-permute-done.1.refs_5_
  54.7 0.0 copy-start.7
  54.7 0.7 copy-done.7
  55.4 5.9 %shard_map.98 = (f32[768,1024]{1,0:T(8,128)}, f32[2,768]{1,0:T(2,128)}) custom-call(s32[768]{0:T(1024)} %doc_ref.13, bf16[768,1024]{1,0:T(8,128)(2,1)} %refs_0_.10, f32[768,1024]{1,0:T(8,128)} %shard_map.96.refs_1_, bf16[768,1024]{1,0:T(8,128)(2,1)} %refs_2_.6, f32[1,1024]{1,0:T(1,128)} %bitcast.1, f32[512,128]{1,0:T(8,128)} %copy-done.5, f32[512,128]{1,0:T(8,128)} %copy-done.7), custom_call_target="tpu_custom_call" | custom-call | flops 201326592 | bytes 9437184 | tf_op jit(solution)/shard_map/pallas_call | solution.py:329
  61.3 2.8 %collective-permute-start.4 = (f32[2,768]{1,0:T(2,128)}, f32[2,768]{1,0:T(2,128)S(1)}, u32[]{:S(2)}, u32[]{:S(2)}) collective-permute-start(f32[2,768]{1,0:T(2,128)} %get-tuple-element.34.refs_4_), channel_id=1, source_target_pairs={{0,3},{1,0},{2,1},{3,2},{4,7},{5,4},{6,5},{7,6},{8,11},{9,8},{10,9... | collective-permute-start | bytes 18440 | tf_op jit(solution)/shard_map/ppermute | solution.py:439
  64.1 0.3 collective-permute-start.3
  64.4 0.7 collective-permute-start.2
  65.1 0.0 collective-permute-done.4.refs_7_
  65.1 0.0 copy-start.8
  65.1 3.1 %collective-permute-done.3.refs_6_ = f32[2,768]{1,0:T(2,128)S(1)} collective-permute-done((f32[2,768]{1,0:T(2,128)}, f32[2,768]{1,0:T(2,128)S(1)}, u32[]{:S(2)}, u32[]{:S(2)}) %collective-permute-start.3) | collective-permute-done | bytes 6176 | tf_op jit(solution)/shard_map/ppermute | solution.py:439
  68.3 0.0 copy-start.9
  68.3 0.1 collective-permute-done.2.refs_5_
  68.3 0.0 copy-start.10
  68.3 0.0 copy-done.8
  68.3 0.5 copy-done.9
  68.9 0.1 copy-done.10
  68.9 6.1 %shard_map.99 = (bf16[768,1024]{1,0:T(8,128)(2,1)}, bf16[768,1024]{1,0:T(8,128)(2,1)}, f32[33,16,128]{2,1,0:T(8,128)}, f32[33,16,128]{2,1,0:T(8,128)}) custom-call(s32[768]{0:T(1024)} %doc_ref.13, f32[768,1024]{1,0:T(8,128)} %get-tuple-element.33.refs_0_, bf16[768,1024]{1,0:T(8,128)(2,1)} %refs_0_.10, bf16[768,1024]{1,0:T(8,128)(2,1)} %refs_2_.6, ...), custom_call_target="tpu_custom_call" | custom-call | flops 201326592 | bytes 10223616 | tf_op jit(solution)/shard_map/pallas_call | solution.py:329
  75.1 2.2 %collective-permute-start.5 = (f32[33,16,128]{2,1,0:T(8,128)}, f32[33,16,128]{2,1,0:T(8,128)S(1)}, u32[]{:S(2)}, u32[]{:S(2)}) collective-permute-start(f32[33,16,128]{2,1,0:T(8,128)} %get-tuple-element.37), channel_id=1, source_target_pairs={{0,4},{4,0},{8,12},{12,8},{16,20},{20,16},{24,28},{28,24},{32,36},... | collective-permute-start | bytes 811016 | tf_op jit(solution)/shard_map/ppermute | solution.py:386
  77.2 1.4 %collective-permute-done.5.refs_1_.refs_2_ = f32[33,16,128]{2,1,0:T(8,128)S(1)} collective-permute-done((f32[33,16,128]{2,1,0:T(8,128)}, f32[33,16,128]{2,1,0:T(8,128)S(1)}, u32[]{:S(2)}, u32[]{:S(2)}) %collective-permute-start.5) | collective-permute-done | bytes 270368 | tf_op jit(solution)/shard_map/ppermute | solution.py:386
  78.6 0.0 copy-start.2
  78.6 1.0 copy-done.2
  79.6 0.8 shard_map.100
  80.3 4.9 %all-to-all-start.2 = ((f32[32,16,128]{2,1,0:T(8,128)}), f32[32,16,128]{2,1,0:T(8,128)S(1)}, u32[]{:S(2)}, u32[]{:S(2)}) async-start(f32[32,16,128]{2,1,0:T(8,128)} %shard_map.100), calls=%async_computation.2 | async-start | bytes 524288 | tf_op jit(solution)/shard_map/all_to_all | solution.py:391
  85.2 11.6 %shard_map.101 = (bf16[768,1024]{1,0:T(8,128)(2,1)}, f32[768,1024]{1,0:T(8,128)}) custom-call(s32[768]{0:T(1024)} %doc_ref.13, bf16[768,1024]{1,0:T(8,128)(2,1)} %refs_0_.10, bf16[768,1024]{1,0:T(8,128)(2,1)} %refs_0_.11, bf16[768,1024]{1,0:T(8,128)(2,1)} %refs_1_.11, bf16[768,1024]{1,0:T(8,128)(2,1)} %get-tuple-element.38.refs_3_.refs_2_, ...), custom_call_target="tpu_custom_call" | custom-call | flops 2617245696 | bytes 11010048 | tf_op jit(solution)/shard_map/pallas_call | solution.py:450
  96.9 0.0 all-to-all-done.2.part_ref
  96.9 0.8 shard_map.102
  97.7 9.0 %all-to-all-start.3 = ((f32[32,16,128]{2,1,0:T(8,128)}), f32[32,16,128]{2,1,0:T(8,128)S(1)}, u32[]{:S(2)}, u32[]{:S(2)}) async-start(f32[32,16,128]{2,1,0:T(8,128)} %shard_map.102), calls=%async_computation.3 | async-start | bytes 524288 | tf_op jit(solution)/shard_map/all_to_all | solution.py:391
  106.7 0.0 copy-start.3
  106.7 7.8 %shard_map.103.refs_3_ = f32[768,1024]{1,0:T(8,128)} custom-call(s32[768]{0:T(1024)} %doc_ref.13, bf16[768,1024]{1,0:T(8,128)(2,1)} %refs_0_.10, bf16[768,1024]{1,0:T(8,128)(2,1)} %refs_0_.11, bf16[768,1024]{1,0:T(8,128)(2,1)} %get-tuple-element.38.refs_3_.refs_2_), custom_call_target="tpu_custom_call" | custom-call | flops 1610612736 | bytes 7864320 | tf_op jit(solution)/shard_map/pallas_call | solution.py:461
  114.6 1.8 %all-to-all-done.3.refs_0_ = f32[32,16,128]{2,1,0:T(8,128)S(1)} async-done(((f32[32,16,128]{2,1,0:T(8,128)}), f32[32,16,128]{2,1,0:T(8,128)S(1)}, u32[]{:S(2)}, u32[]{:S(2)}) %all-to-all-start.3) | async-done | bytes 262176 | tf_op jit(solution)/shard_map/all_to_all | solution.py:391
  116.4 0.0 copy-done.3
  116.4 0.1 shard_map.104
  116.4 0.0 copy-start.4
  116.4 0.7 copy-done.4
  117.1 3.6 %collective-permute-start.6 = (f32[512,128]{1,0:T(8,128)S(1)}, f32[512,128]{1,0:T(8,128)S(1)}, u32[]{:S(2)}, u32[]{:S(2)}) collective-permute-start(f32[512,128]{1,0:T(8,128)S(1)} %get-tuple-element.47), channel_id=1, source_target_pairs={{0,4},{4,0},{8,12},{12,8},{16,20},{20,16},{24,28},{28,24},{32,36},... | collective-permute-start | bytes 786440 | tf_op jit(solution)/shard_map/ppermute | solution.py:386
  120.7 1.2 collective-permute-done.6.refs_5_
  121.9 0.0 copy-start.6
  121.9 0.7 copy-done.6
  122.6 6.8 %shard_map.105 = (bf16[768,1024]{1,0:T(8,128)(2,1)}, bf16[768,1024]{1,0:T(8,128)(2,1)}) custom-call(s32[768]{0:T(1024)} %doc_ref.13, bf16[768,1024]{1,0:T(8,128)(2,1)} %refs_0_.11, bf16[768,1024]{1,0:T(8,128)(2,1)} %refs_1_.11, f32[768,1024]{1,0:T(8,128)} %get-tuple-element.42.refs_2_, f32[768,1024]{1,0:T(8,128)} %shard_map.103.refs_3_, ...), custom_call_target="tpu_custom_call" | custom-call | flops 402653184 | bytes 12582912 | tf_op jit(solution)/shard_map/pallas_call | solution.py:329
Async XLA Ops:
  4.5 4.7 %collective-permute-start = (f32[33,16,128]{2,1,0:T(8,128)}, f32[33,16,128]{2,1,0:T(8,128)S(1)}, u32[]{:S(2)}, u32[]{:S(2)}) collective-permute-start(f32[33,16,128]{2,1,0:T(8,128)} %get-tuple-element.28), channel_id=1, source_target_pairs={{0,4},{4,0},{8,12},{12,8},{16,20},{20,16},{24,28},{28,24},{32,36},... | collective-permute-start | bytes 811016 | tf_op jit(solution)/shard_map/ppermute | solution.py:386
  9.2 1.0 copy-start
  31.9 17.2 %all-to-all-start.1 = ((f32[32,16,128]{2,1,0:T(8,128)}), f32[32,16,128]{2,1,0:T(8,128)S(1)}, u32[]{:S(2)}, u32[]{:S(2)}) async-start(f32[32,16,128]{2,1,0:T(8,128)} %shard_map.95), calls=%async_computation.1 | async-start | bytes 524288 | tf_op jit(solution)/shard_map/all_to_all | solution.py:391
  39.4 9.7 %copy-start.1 = (f32[33,16,128]{2,1,0:T(8,128)S(1)}, f32[33,16,128]{2,1,0:T(8,128)}, u32[]{:S(2)}) copy-start(f32[33,16,128]{2,1,0:T(8,128)} %get-tuple-element.27.refs_0_.refs_1_) | copy-start | bytes 811012
  49.2 0.7 copy-start.5
  49.9 4.8 %collective-permute-start.1 = (f32[512,128]{1,0:T(8,128)S(1)}, f32[512,128]{1,0:T(8,128)S(1)}, u32[]{:S(2)}, u32[]{:S(2)}) collective-permute-start(f32[512,128]{1,0:T(8,128)S(1)} %get-tuple-element.32), channel_id=1, source_target_pairs={{0,4},{4,0},{8,12},{12,8},{16,20},{20,16},{24,28},{28,24},{32,36},... | collective-permute-start | bytes 786440 | tf_op jit(solution)/shard_map/ppermute | solution.py:386
  54.7 0.7 copy-start.7
  61.3 3.9 %collective-permute-start.4 = (f32[2,768]{1,0:T(2,128)}, f32[2,768]{1,0:T(2,128)S(1)}, u32[]{:S(2)}, u32[]{:S(2)}) collective-permute-start(f32[2,768]{1,0:T(2,128)} %get-tuple-element.34.refs_4_), channel_id=1, source_target_pairs={{0,3},{1,0},{2,1},{3,2},{4,7},{5,4},{6,5},{7,6},{8,11},{9,8},{10,9... | collective-permute-start | bytes 18440 | tf_op jit(solution)/shard_map/ppermute | solution.py:439
  64.1 4.2 %collective-permute-start.3 = (f32[2,768]{1,0:T(2,128)}, f32[2,768]{1,0:T(2,128)S(1)}, u32[]{:S(2)}, u32[]{:S(2)}) collective-permute-start(f32[2,768]{1,0:T(2,128)} %get-tuple-element.34.refs_4_), channel_id=1, source_target_pairs={{0,2},{1,3},{2,0},{3,1},{4,6},{5,7},{6,4},{7,5},{8,10},{9,11},{10,... | collective-permute-start | bytes 18440 | tf_op jit(solution)/shard_map/ppermute | solution.py:439
  64.4 3.9 %collective-permute-start.2 = (f32[2,768]{1,0:T(2,128)}, f32[2,768]{1,0:T(2,128)S(1)}, u32[]{:S(2)}, u32[]{:S(2)}) collective-permute-start(f32[2,768]{1,0:T(2,128)} %get-tuple-element.34.refs_4_), channel_id=1, source_target_pairs={{0,1},{1,2},{2,3},{3,0},{4,5},{5,6},{6,7},{7,4},{8,9},{9,10},{10,1... | collective-permute-start | bytes 18440 | tf_op jit(solution)/shard_map/ppermute | solution.py:439
  65.1 3.2 %copy-start.8 = (f32[2,768]{1,0:T(2,128)}, f32[2,768]{1,0:T(2,128)S(1)}, u32[]{:S(2)}) copy-start(f32[2,768]{1,0:T(2,128)S(1)} %collective-permute-done.4.refs_7_) | copy-start | bytes 18436
  68.3 0.6 copy-start.9
  68.3 0.6 copy-start.10
  75.1 3.5 %collective-permute-start.5 = (f32[33,16,128]{2,1,0:T(8,128)}, f32[33,16,128]{2,1,0:T(8,128)S(1)}, u32[]{:S(2)}, u32[]{:S(2)}) collective-permute-start(f32[33,16,128]{2,1,0:T(8,128)} %get-tuple-element.37), channel_id=1, source_target_pairs={{0,4},{4,0},{8,12},{12,8},{16,20},{20,16},{24,28},{28,24},{32,36},... | collective-permute-start | bytes 811016 | tf_op jit(solution)/shard_map/ppermute | solution.py:386
  78.6 1.0 copy-start.2
  80.3 16.5 %all-to-all-start.2 = ((f32[32,16,128]{2,1,0:T(8,128)}), f32[32,16,128]{2,1,0:T(8,128)S(1)}, u32[]{:S(2)}, u32[]{:S(2)}) async-start(f32[32,16,128]{2,1,0:T(8,128)} %shard_map.100), calls=%async_computation.2 | async-start | bytes 524288 | tf_op jit(solution)/shard_map/all_to_all | solution.py:391
  97.7 18.7 %all-to-all-start.3 = ((f32[32,16,128]{2,1,0:T(8,128)}), f32[32,16,128]{2,1,0:T(8,128)S(1)}, u32[]{:S(2)}, u32[]{:S(2)}) async-start(f32[32,16,128]{2,1,0:T(8,128)} %shard_map.102), calls=%async_computation.3 | async-start | bytes 524288 | tf_op jit(solution)/shard_map/all_to_all | solution.py:391
  106.7 9.7 %copy-start.3 = (f32[33,16,128]{2,1,0:T(8,128)S(1)}, f32[33,16,128]{2,1,0:T(8,128)}, u32[]{:S(2)}) copy-start(f32[33,16,128]{2,1,0:T(8,128)} %get-tuple-element.36.refs_0_.refs_1_) | copy-start | bytes 811012
  116.4 0.7 copy-start.4
  117.1 4.8 %collective-permute-start.6 = (f32[512,128]{1,0:T(8,128)S(1)}, f32[512,128]{1,0:T(8,128)S(1)}, u32[]{:S(2)}, u32[]{:S(2)}) collective-permute-start(f32[512,128]{1,0:T(8,128)S(1)} %get-tuple-element.47), channel_id=1, source_target_pairs={{0,4},{4,0},{8,12},{12,8},{16,20},{20,16},{24,28},{28,24},{32,36},... | collective-permute-start | bytes 786440 | tf_op jit(solution)/shard_map/ppermute | solution.py:386
  121.9 0.7 copy-start.6

commit v4 on v3

--- a/solution.py
+++ b/solution.py
@@ -254,9 +254,9 @@
                 out_ref[rows_from(s), columns(h)] += part
 
 
-def back_kernel(heads, doc_ref, place_ref, query_ref, key_ref, value_ref, grad_ref, mine_ref,
-                theirs_ref, grad_q_ref, key_part_ref, grad_q):
-    units = query_ref.shape[0] // UNIT
+def back_kernel(heads, doc_ref, place_ref, key_ref, value_ref, grad_ref, mine_ref, theirs_ref,
+                grad_q_ref, grad_q):
+    units = key_ref.shape[0] // UNIT
     for h in range(heads):
         prefix = pick(place_ref, mine_ref, theirs_ref, h)
         for t in range(units):
@@ -265,18 +265,20 @@
         for s in range(units):
             backs = lower_scores(doc_ref, grad_ref, value_ref, s, h)
             grad_q[rows_from(s), columns(h)] += dot(backs, key_ref[unit(s), columns(h)], (1, 0))
-            key_part_ref[unit(s), columns(h)] = dot(
-                backs, query_ref[rows_from(s), columns(h)], (0, 0)
-            )
         grad_q_ref[:, columns(h)] = grad_q[:, columns(h)].astype(BF16)
 
 
-def value_kernel(heads, doc_ref, query_ref, key_ref, grad_ref, value_part_ref):
+def parts_kernel(heads, doc_ref, query_ref, key_ref, value_ref, grad_ref, key_part_ref,
+                 value_part_ref):
     for h in range(heads):
         for s in range(query_ref.shape[0] // UNIT):
             attend = upper_scores(doc_ref, key_ref, query_ref, s, h)
             value_part_ref[unit(s), columns(h)] = dot(
                 attend, grad_ref[rows_from(s), columns(h)], (1, 0)
+            )
+            backs = upper_scores(doc_ref, value_ref, grad_ref, s, h)
+            key_part_ref[unit(s), columns(h)] = dot(
+                backs, query_ref[rows_from(s), columns(h)], (1, 0)
             )
 
 
@@ -447,26 +449,26 @@
 
     received = sibling(theirs)
     gathered = exchange(combine(1, mine, received, SLICE))
-    grad_q, key_part = call(
+    (grad_q,) = call(
         functools.partial(back_kernel, per_step),
-        [wide] * 4 + [halves, halves],
+        [wide] * 3 + [halves, halves],
+        [wide],
+        [narrow],
+        2 * 512 + HEAD_DIM,
+        8,
+        [pltpu.VMEM((tokens, step_cols), F32)],
+    )(keys, values, grad_out, *prefix)
+    gathered, grad_q = lax.optimization_barrier((gathered, grad_q))
+    entering = exchange(scan(gathered, flags, True))
+    parts = call(
+        placeless(functools.partial(parts_kernel, per_step)),
+        [wide] * 4,
         [wide] * 2,
-        [narrow, tall],
-        3 * 512 + HEAD_DIM,
-        14,
-        [pltpu.VMEM((tokens, step_cols), F32)],
-    )(queries, keys, values, grad_out, *prefix)
-    gathered, grad_q, key_part = lax.optimization_barrier((gathered, grad_q, key_part))
-    entering = exchange(scan(gathered, flags, True))
-    value_part = call(
-        placeless(functools.partial(value_kernel, per_step)),
-        [wide] * 3,
-        wide,
-        tall,
-        2 * 512,
-        10,
-    )(queries, keys, grad_out)
-    entering, value_part = lax.optimization_barrier((entering, value_part))
+        [tall, tall],
+        4 * 512,
+        16,
+    )(queries, keys, values, grad_out)
+    entering, key_part, value_part = lax.optimization_barrier((entering, *parts))
     suffix = spread(1, entering, mine, received)
 
     grad_k, grad_v = stream(

time: 130 us -> 126 us (0.969)
  starting transfers between devices: 38 us -> 33.9 us
    ppermute x4, starting transfers between devices: 12.7 us -> 10.5 us  [sibling(): return lax.ppermute(data, 'seq', [(i, i ^ 1) for i in range(blocks)])]
    all_to_all x3, starting transfers between devices: 21.5 us -> 19.6 us  [exchange(): return lax.all_to_all(data, 'seq', 0, 0, axis_index_groups=groups)]
where the time goes in v4:
time: 126 us
  Pallas kernels  51.8 us (41%)
  starting transfers between devices  33.9 us (27%)
  blocking collectives  20.9 us (17%)
  waiting for transfers between devices  12.6 us (10%)
  local copies, waits for them, and re-layouts  5.34 us (4%)
    pallas_call x4, Pallas kernels, stream(): pl.pallas_call(body, in_specs=[docs] + [anywhere] * ins + [vmem] * len(op...  22.6 us
    all_to_all x1, blocking collectives, exchange(): return lax.all_to_all(data, 'seq', 0, 0, axis_index_groups=groups)  20.9 us
    all_to_all x3, starting transfers between devices, exchange(): return lax.all_to_all(data, 'seq', 0, 0, axis_index_groups=groups)  19.6 us
    pallas_call x1, Pallas kernels, on_device(): call(placeless(functools.partial(parts_kernel, per_step)), [wide] * 4, [w...  11.9 us
    ppermute x4, starting transfers between devices, sibling(): return lax.ppermute(data, 'seq', [(i, i ^ 1) for i in range(blocks)])  10.5 us
    pallas_call x1, Pallas kernels, on_device(): call(functools.partial(back_kernel, per_step), [wide] * 3 + [halves, halv...  7.62 us
    pallas_call x1, Pallas kernels, on_device(): call(placeless(functools.partial(local_kernel, per_step)), [wide] * 3, wi...  7.19 us
    unnamed x22, local copies, waits for them, and re-layouts  5.34 us
  transfers between devices with their start and end apart: 10, of which 8 were waited for; matrix products, arithmetic and copies ran while one was open for 0% of the time, Pallas kernels for 21%

profile of v4, /device:TPU:1, one launch (start us, length us, event | category | flops | bytes accessed | tf_op | source)
XLA Modules:
  0.0 125.5 jit_solution(5057355418662444695)
XLA Ops:
  0.6 3.8 %shard_map.93 = (f32[33,16,128]{2,1,0:T(8,128)}, f32[33,16,128]{2,1,0:T(8,128)}) custom-call(s32[768]{0:T(1024)} %doc_ref.13, bf16[768,1024]{1,0:T(8,128)(2,1)} %refs_0_.11, bf16[768,1024]{1,0:T(8,128)(2,1)} %refs_1_.11), custom_call_target="tpu_custom_call" | custom-call | flops 201326592 | bytes 3932160 | tf_op jit(solution)/shard_map/pallas_call | solution.py:331
  4.5 3.3 %collective-permute-start = (f32[33,16,128]{2,1,0:T(8,128)}, f32[33,16,128]{2,1,0:T(8,128)S(1)}, u32[]{:S(2)}, u32[]{:S(2)}) collective-permute-start(f32[33,16,128]{2,1,0:T(8,128)} %get-tuple-element.28), channel_id=1, source_target_pairs={{0,4},{4,0},{8,12},{12,8},{16,20},{20,16},{24,28},{28,24},{32,36},... | collective-permute-start | bytes 811016 | tf_op jit(solution)/shard_map/ppermute | solution.py:388
  7.8 1.4 %collective-permute-done.refs_1_.refs_2_ = f32[33,16,128]{2,1,0:T(8,128)S(1)} collective-permute-done((f32[33,16,128]{2,1,0:T(8,128)}, f32[33,16,128]{2,1,0:T(8,128)S(1)}, u32[]{:S(2)}, u32[]{:S(2)}) %collective-permute-start) | collective-permute-done | bytes 270368 | tf_op jit(solution)/shard_map/ppermute | solution.py:388
  9.2 0.0 copy-start
  9.2 1.0 copy-done
  10.1 0.1 shard_map.94
  10.2 20.9 %all_to_all.20.part_ref.flag_ref = f32[32,24,128]{2,1,0:T(8,128)S(1)} all-to-all(f32[32,24,128]{2,1,0:T(8,128)S(1)} %shard_map.94), channel_id=1, replica_groups={{0,8,16,24,32,40,48,56,64,72,80,88,96,104,112,120,128,136,144,152,160,1..., dimensions={0} | all-to-all | bytes 786432 | tf_op jit(solution)/shard_map/all_to_all | solution.py:393
  31.1 0.8 shard_map.95
  31.9 7.6 %all-to-all-start.1 = ((f32[32,16,128]{2,1,0:T(8,128)}), f32[32,16,128]{2,1,0:T(8,128)S(1)}, u32[]{:S(2)}, u32[]{:S(2)}) async-start(f32[32,16,128]{2,1,0:T(8,128)} %shard_map.95), calls=%async_computation.1 | async-start | bytes 524288 | tf_op jit(solution)/shard_map/all_to_all | solution.py:393
  39.4 0.0 copy-start.1
  39.4 7.2 %shard_map.96.refs_1_ = f32[768,1024]{1,0:T(8,128)} custom-call(s32[768]{0:T(1024)} %doc_ref.13, bf16[768,1024]{1,0:T(8,128)(2,1)} %refs_0_.10, bf16[768,1024]{1,0:T(8,128)(2,1)} %refs_0_.11, bf16[768,1024]{1,0:T(8,128)(2,1)} %refs_1_.11), custom_call_target="tpu_custom_call" | custom-call | flops 1610612736 | bytes 7864320 | tf_op jit(solution)/shard_map/pallas_call | solution.py:422
  46.6 2.5 %all-to-all-done.1.refs_0_ = f32[32,16,128]{2,1,0:T(8,128)S(1)} async-done(((f32[32,16,128]{2,1,0:T(8,128)}), f32[32,16,128]{2,1,0:T(8,128)S(1)}, u32[]{:S(2)}, u32[]{:S(2)}) %all-to-all-start.1) | async-done | bytes 262176 | tf_op jit(solution)/shard_map/all_to_all | solution.py:393
  49.1 0.0 copy-done.1
  49.1 0.1 shard_map.97
  49.2 0.0 copy-start.4
  49.2 0.7 copy-done.4
  49.9 3.6 %collective-permute-start.1 = (f32[512,128]{1,0:T(8,128)S(1)}, f32[512,128]{1,0:T(8,128)S(1)}, u32[]{:S(2)}, u32[]{:S(2)}) collective-permute-start(f32[512,128]{1,0:T(8,128)S(1)} %get-tuple-element.32), channel_id=1, source_target_pairs={{0,4},{4,0},{8,12},{12,8},{16,20},{20,16},{24,28},{28,24},{32,36},... | collective-permute-start | bytes 786440 | tf_op jit(solution)/shard_map/ppermute | solution.py:388
  53.5 1.2 collective-permute-done.1.refs_5_.refs_4_
  54.7 0.0 copy-start.6
  54.7 0.7 copy-done.6
  55.4 5.9 %shard_map.98 = (f32[768,1024]{1,0:T(8,128)}, f32[2,768]{1,0:T(2,128)}) custom-call(s32[768]{0:T(1024)} %doc_ref.13, bf16[768,1024]{1,0:T(8,128)(2,1)} %refs_0_.10, f32[768,1024]{1,0:T(8,128)} %shard_map.96.refs_1_, bf16[768,1024]{1,0:T(8,128)(2,1)} %refs_2_.6, f32[1,1024]{1,0:T(1,128)} %bitcast.1, f32[512,128]{1,0:T(8,128)} %copy-done.4, f32[512,128]{1,0:T(8,128)} %copy-done.6), custom_call_target="tpu_custom_call" | custom-call | flops 201326592 | bytes 9437184 | tf_op jit(solution)/shard_map/pallas_call | solution.py:331
  61.3 2.8 %collective-permute-start.4 = (f32[2,768]{1,0:T(2,128)}, f32[2,768]{1,0:T(2,128)S(1)}, u32[]{:S(2)}, u32[]{:S(2)}) collective-permute-start(f32[2,768]{1,0:T(2,128)} %get-tuple-element.34.refs_4_), channel_id=1, source_target_pairs={{0,3},{1,0},{2,1},{3,2},{4,7},{5,4},{6,5},{7,6},{8,11},{9,8},{10,9... | collective-permute-start | bytes 18440 | tf_op jit(solution)/shard_map/ppermute | solution.py:441
  64.1 0.3 collective-permute-start.3
  64.4 0.7 collective-permute-start.2
  65.1 0.0 collective-permute-done.4.refs_7_
  65.1 0.0 copy-start.8
  65.1 3.1 %collective-permute-done.3.refs_6_ = f32[2,768]{1,0:T(2,128)S(1)} collective-permute-done((f32[2,768]{1,0:T(2,128)}, f32[2,768]{1,0:T(2,128)S(1)}, u32[]{:S(2)}, u32[]{:S(2)}) %collective-permute-start.3) | collective-permute-done | bytes 6176 | tf_op jit(solution)/shard_map/ppermute | solution.py:441
  68.3 0.0 copy-start.9
  68.3 0.1 collective-permute-done.2.refs_5_
  68.3 0.0 copy-start.10
  68.3 0.0 copy-done.8
  68.3 0.5 copy-done.9
  68.9 0.1 copy-done.10
  68.9 6.1 %shard_map.99 = (bf16[768,1024]{1,0:T(8,128)(2,1)}, bf16[768,1024]{1,0:T(8,128)(2,1)}, f32[33,16,128]{2,1,0:T(8,128)}, f32[33,16,128]{2,1,0:T(8,128)}) custom-call(s32[768]{0:T(1024)} %doc_ref.13, f32[768,1024]{1,0:T(8,128)} %get-tuple-element.33.refs_0_, bf16[768,1024]{1,0:T(8,128)(2,1)} %refs_0_.10, bf16[768,1024]{1,0:T(8,128)(2,1)} %refs_2_.6, ...), custom_call_target="tpu_custom_call" | custom-call | flops 201326592 | bytes 10223616 | tf_op jit(solution)/shard_map/pallas_call | solution.py:331
  75.1 2.2 %collective-permute-start.5 = (f32[33,16,128]{2,1,0:T(8,128)}, f32[33,16,128]{2,1,0:T(8,128)S(1)}, u32[]{:S(2)}, u32[]{:S(2)}) collective-permute-start(f32[33,16,128]{2,1,0:T(8,128)} %get-tuple-element.37), channel_id=1, source_target_pairs={{0,4},{4,0},{8,12},{12,8},{16,20},{20,16},{24,28},{28,24},{32,36},... | collective-permute-start | bytes 811016 | tf_op jit(solution)/shard_map/ppermute | solution.py:388
  77.2 1.4 %collective-permute-done.5.refs_1_.refs_2_ = f32[33,16,128]{2,1,0:T(8,128)S(1)} collective-permute-done((f32[33,16,128]{2,1,0:T(8,128)}, f32[33,16,128]{2,1,0:T(8,128)S(1)}, u32[]{:S(2)}, u32[]{:S(2)}) %collective-permute-start.5) | collective-permute-done | bytes 270368 | tf_op jit(solution)/shard_map/ppermute | solution.py:388
  78.6 0.0 copy-start.2
  78.6 1.0 copy-done.2
  79.6 0.8 shard_map.100
  80.3 4.9 %all-to-all-start.2 = ((f32[32,16,128]{2,1,0:T(8,128)}), f32[32,16,128]{2,1,0:T(8,128)S(1)}, u32[]{:S(2)}, u32[]{:S(2)}) async-start(f32[32,16,128]{2,1,0:T(8,128)} %shard_map.100), calls=%async_computation.2 | async-start | bytes 524288 | tf_op jit(solution)/shard_map/all_to_all | solution.py:393
  85.2 7.6 %shard_map.101 = bf16[768,1024]{1,0:T(8,128)(2,1)} custom-call(s32[768]{0:T(1024)} %doc_ref.13, bf16[768,1024]{1,0:T(8,128)(2,1)} %refs_0_.11, bf16[768,1024]{1,0:T(8,128)(2,1)} %refs_1_.11, bf16[768,1024]{1,0:T(8,128)(2,1)} %get-tuple-element.38.refs_2_.refs_3_, f32[512,128]{1,0:T(8,128)} %copy-done.4, f32[512,128]{1,0:T(8,128)} %copy-done.6), custom_call_target="tpu_custom_call" | custom-call | flops 1811939328 | bytes 6291456 | tf_op jit(solution)/shard_map/pallas_call | solution.py:452
  92.9 1.9 %all-to-all-done.2.part_ref = f32[32,16,128]{2,1,0:T(8,128)S(1)} async-done(((f32[32,16,128]{2,1,0:T(8,128)}), f32[32,16,128]{2,1,0:T(8,128)S(1)}, u32[]{:S(2)}, u32[]{:S(2)}) %all-to-all-start.2) | async-done | bytes 262176 | tf_op jit(solution)/shard_map/all_to_all | solution.py:393
  94.7 0.8 shard_map.102
  95.5 7.2 %all-to-all-start.3 = ((f32[32,16,128]{2,1,0:T(8,128)}), f32[32,16,128]{2,1,0:T(8,128)S(1)}, u32[]{:S(2)}, u32[]{:S(2)}) async-start(f32[32,16,128]{2,1,0:T(8,128)} %shard_map.102), calls=%async_computation.3 | async-start | bytes 524288 | tf_op jit(solution)/shard_map/all_to_all | solution.py:393
  102.7 0.0 copy-start.3
  102.7 11.9 %shard_map.103 = (f32[768,1024]{1,0:T(8,128)}, f32[768,1024]{1,0:T(8,128)}) custom-call(s32[768]{0:T(1024)} %doc_ref.13, bf16[768,1024]{1,0:T(8,128)(2,1)} %refs_0_.10, bf16[768,1024]{1,0:T(8,128)(2,1)} %refs_0_.11, bf16[768,1024]{1,0:T(8,128)(2,1)} %refs_1_.11, bf16[768,1024]{1,0:T(8,128)(2,1)} %get-tuple-element.38.refs_2_.refs_3_), custom_call_target="tpu_custom_call" | custom-call | flops 3221225472 | bytes 12582912 | tf_op jit(solution)/shard_map/pallas_call | solution.py:463
  114.6 0.0 all-to-all-done.3.refs_0_
  114.6 0.0 copy-done.3
  114.6 0.1 shard_map.104
  114.7 0.0 copy-start.5
  114.7 0.7 copy-done.5
  115.4 1.4 %collective-permute-start.6 = (f32[512,128]{1,0:T(8,128)S(1)}, f32[512,128]{1,0:T(8,128)S(1)}, u32[]{:S(2)}, u32[]{:S(2)}) collective-permute-start(f32[512,128]{1,0:T(8,128)S(1)} %get-tuple-element.47), channel_id=1, source_target_pairs={{0,4},{4,0},{8,12},{12,8},{16,20},{20,16},{24,28},{28,24},{32,36},... | collective-permute-start | bytes 786440 | tf_op jit(solution)/shard_map/ppermute | solution.py:388
  116.7 1.2 collective-permute-done.6.refs_5_
  117.9 0.0 copy-start.7
  117.9 0.7 copy-done.7
  118.6 6.8 %shard_map.105 = (bf16[768,1024]{1,0:T(8,128)(2,1)}, bf16[768,1024]{1,0:T(8,128)(2,1)}) custom-call(s32[768]{0:T(1024)} %doc_ref.13, bf16[768,1024]{1,0:T(8,128)(2,1)} %refs_0_.11, bf16[768,1024]{1,0:T(8,128)(2,1)} %refs_1_.11, f32[768,1024]{1,0:T(8,128)} %get-tuple-element.43.refs_2_, f32[768,1024]{1,0:T(8,128)} %get-tuple-element.44.refs_3_, ...), custom_call_target="tpu_custom_call" | custom-call | flops 402653184 | bytes 12582912 | tf_op jit(solution)/shard_map/pallas_call | solution.py:331
Async XLA Ops:
  4.5 4.7 %collective-permute-start = (f32[33,16,128]{2,1,0:T(8,128)}, f32[33,16,128]{2,1,0:T(8,128)S(1)}, u32[]{:S(2)}, u32[]{:S(2)}) collective-permute-start(f32[33,16,128]{2,1,0:T(8,128)} %get-tuple-element.28), channel_id=1, source_target_pairs={{0,4},{4,0},{8,12},{12,8},{16,20},{20,16},{24,28},{28,24},{32,36},... | collective-permute-start | bytes 811016 | tf_op jit(solution)/shard_map/ppermute | solution.py:388
  9.2 1.0 copy-start
  31.9 17.2 %all-to-all-start.1 = ((f32[32,16,128]{2,1,0:T(8,128)}), f32[32,16,128]{2,1,0:T(8,128)S(1)}, u32[]{:S(2)}, u32[]{:S(2)}) async-start(f32[32,16,128]{2,1,0:T(8,128)} %shard_map.95), calls=%async_computation.1 | async-start | bytes 524288 | tf_op jit(solution)/shard_map/all_to_all | solution.py:393
  39.4 9.7 %copy-start.1 = (f32[33,16,128]{2,1,0:T(8,128)S(1)}, f32[33,16,128]{2,1,0:T(8,128)}, u32[]{:S(2)}) copy-start(f32[33,16,128]{2,1,0:T(8,128)} %get-tuple-element.27.refs_0_.refs_1_) | copy-start | bytes 811012
  49.2 0.7 copy-start.4
  49.9 4.8 %collective-permute-start.1 = (f32[512,128]{1,0:T(8,128)S(1)}, f32[512,128]{1,0:T(8,128)S(1)}, u32[]{:S(2)}, u32[]{:S(2)}) collective-permute-start(f32[512,128]{1,0:T(8,128)S(1)} %get-tuple-element.32), channel_id=1, source_target_pairs={{0,4},{4,0},{8,12},{12,8},{16,20},{20,16},{24,28},{28,24},{32,36},... | collective-permute-start | bytes 786440 | tf_op jit(solution)/shard_map/ppermute | solution.py:388
  54.7 0.7 copy-start.6
  61.3 3.9 %collective-permute-start.4 = (f32[2,768]{1,0:T(2,128)}, f32[2,768]{1,0:T(2,128)S(1)}, u32[]{:S(2)}, u32[]{:S(2)}) collective-permute-start(f32[2,768]{1,0:T(2,128)} %get-tuple-element.34.refs_4_), channel_id=1, source_target_pairs={{0,3},{1,0},{2,1},{3,2},{4,7},{5,4},{6,5},{7,6},{8,11},{9,8},{10,9... | collective-permute-start | bytes 18440 | tf_op jit(solution)/shard_map/ppermute | solution.py:441
  64.1 4.2 %collective-permute-start.3 = (f32[2,768]{1,0:T(2,128)}, f32[2,768]{1,0:T(2,128)S(1)}, u32[]{:S(2)}, u32[]{:S(2)}) collective-permute-start(f32[2,768]{1,0:T(2,128)} %get-tuple-element.34.refs_4_), channel_id=1, source_target_pairs={{0,2},{1,3},{2,0},{3,1},{4,6},{5,7},{6,4},{7,5},{8,10},{9,11},{10,... | collective-permute-start | bytes 18440 | tf_op jit(solution)/shard_map/ppermute | solution.py:441
  64.4 3.9 %collective-permute-start.2 = (f32[2,768]{1,0:T(2,128)}, f32[2,768]{1,0:T(2,128)S(1)}, u32[]{:S(2)}, u32[]{:S(2)}) collective-permute-start(f32[2,768]{1,0:T(2,128)} %get-tuple-element.34.refs_4_), channel_id=1, source_target_pairs={{0,1},{1,2},{2,3},{3,0},{4,5},{5,6},{6,7},{7,4},{8,9},{9,10},{10,1... | collective-permute-start | bytes 18440 | tf_op jit(solution)/shard_map/ppermute | solution.py:441
  65.1 3.2 %copy-start.8 = (f32[2,768]{1,0:T(2,128)}, f32[2,768]{1,0:T(2,128)S(1)}, u32[]{:S(2)}) copy-start(f32[2,768]{1,0:T(2,128)S(1)} %collective-permute-done.4.refs_7_) | copy-start | bytes 18436
  68.3 0.6 copy-start.9
  68.3 0.6 copy-start.10
  75.1 3.5 %collective-permute-start.5 = (f32[33,16,128]{2,1,0:T(8,128)}, f32[33,16,128]{2,1,0:T(8,128)S(1)}, u32[]{:S(2)}, u32[]{:S(2)}) collective-permute-start(f32[33,16,128]{2,1,0:T(8,128)} %get-tuple-element.37), channel_id=1, source_target_pairs={{0,4},{4,0},{8,12},{12,8},{16,20},{20,16},{24,28},{28,24},{32,36},... | collective-permute-start | bytes 811016 | tf_op jit(solution)/shard_map/ppermute | solution.py:388
  78.6 1.0 copy-start.2
  80.3 14.4 %all-to-all-start.2 = ((f32[32,16,128]{2,1,0:T(8,128)}), f32[32,16,128]{2,1,0:T(8,128)S(1)}, u32[]{:S(2)}, u32[]{:S(2)}) async-start(f32[32,16,128]{2,1,0:T(8,128)} %shard_map.100), calls=%async_computation.2 | async-start | bytes 524288 | tf_op jit(solution)/shard_map/all_to_all | solution.py:393
  95.5 19.1 %all-to-all-start.3 = ((f32[32,16,128]{2,1,0:T(8,128)}), f32[32,16,128]{2,1,0:T(8,128)S(1)}, u32[]{:S(2)}, u32[]{:S(2)}) async-start(f32[32,16,128]{2,1,0:T(8,128)} %shard_map.102), calls=%async_computation.3 | async-start | bytes 524288 | tf_op jit(solution)/shard_map/all_to_all | solution.py:393
  102.7 11.9 %copy-start.3 = (f32[33,16,128]{2,1,0:T(8,128)S(1)}, f32[33,16,128]{2,1,0:T(8,128)}, u32[]{:S(2)}) copy-start(f32[33,16,128]{2,1,0:T(8,128)} %get-tuple-element.36.refs_0_.refs_1_) | copy-start | bytes 811012
  114.7 0.7 copy-start.5
  115.4 2.5 %collective-permute-start.6 = (f32[512,128]{1,0:T(8,128)S(1)}, f32[512,128]{1,0:T(8,128)S(1)}, u32[]{:S(2)}, u32[]{:S(2)}) collective-permute-start(f32[512,128]{1,0:T(8,128)S(1)} %get-tuple-element.47), channel_id=1, source_target_pairs={{0,4},{4,0},{8,12},{12,8},{16,20},{20,16},{24,28},{28,24},{32,36},... | collective-permute-start | bytes 786440 | tf_op jit(solution)/shard_map/ppermute | solution.py:388
  117.9 0.7 copy-start.7
